TPU v7x, 32 devices: a whole 2x2x4 slice. The times are simulated.
32 devices in a mesh: ctx: 4 (over y, x), fsdp: 8 (over z, core).
Axes of the slice: x: 2, y: 2, z: 4, core: 2. Of those that a mesh axis runs over, the one named last changes fastest.
Arguments:
- layer_input: bfloat16 [2, 8, 1024, 1088], P(None, 'fsdp', 'ctx'), may hold values from -6 to 6
- output_grad: bfloat16 [2, 8, 1024, 1088], P(None, 'fsdp', 'ctx'), may hold values from -6 to 6
- attn_gain: bfloat16 [1088], P('fsdp'), may hold values from 0.5 to 1.5
- attn_shift: bfloat16 [1088], P('fsdp'), may hold values from -1 to 1
- merged_weight: bfloat16 [1088, 3264], P('fsdp'), may hold values from -0.1875 to 0.1875
- query_bias: bfloat16 [1088], P('fsdp'), may hold values from -2.5 to 2.5
- value_bias: bfloat16 [1088], P('fsdp'), may hold values from -1.5 to 1.5
- out_weight: bfloat16 [1088, 1088], P('fsdp'), may hold values from -3 to 3
- out_bias: bfloat16 [1088], P('fsdp'), may hold values from -1 to 1
- mlp_gain: bfloat16 [1088], P('fsdp'), may hold values from 0.5 to 1.5
- mlp_shift: bfloat16 [1088], P('fsdp'), may hold values from -1 to 1
- up_weight: bfloat16 [1088, 4352], P('fsdp'), may hold values from -0.1875 to 0.1875
- up_bias: bfloat16 [4352], P('fsdp'), may hold values from -1.5 to 1.5
- down_weight: bfloat16 [4352, 1088], P('fsdp'), may hold values from -0.1875 to 0.1875
- down_bias: bfloat16 [1088], P('fsdp'), may hold values from -1 to 1
Outputs:
- layer_output: bfloat16 [2, 8, 1024, 1088], P(None, 'fsdp', 'ctx')
- input_grad: float32 [2, 8, 1024, 1088], P(None, 'fsdp', 'ctx')
- grad_attn_gain: float32 [1088], P('fsdp')
- grad_attn_shift: float32 [1088], P('fsdp')
- grad_merged_weight: float32 [1088, 3264], P('fsdp')
- grad_query_bias: float32 [1088], P('fsdp')
- grad_value_bias: float32 [1088], P('fsdp')
- grad_out_weight: float32 [1088, 1088], P('fsdp')
- grad_out_bias: float32 [1088], P('fsdp')
- grad_mlp_gain: float32 [1088], P('fsdp')
- grad_mlp_shift: float32 [1088], P('fsdp')
- grad_up_weight: float32 [1088, 4352], P('fsdp')
- grad_up_bias: float32 [4352], P('fsdp')
- grad_down_weight: float32 [4352, 1088], P('fsdp')
- grad_down_bias: float32 [1088], P('fsdp')
All inputs are finite; a program needn't handle non-finite values.
Results may differ from a plain program's by a relative error of at most 0.02.
Values may be sent and summed in bfloat16 or wider, within the bound.
No kernel may reach another device: no remote copies, remote signals or barrier semaphores. Data moves between devices by JAX's collectives and lax.ppermute only.
A program may use at most 256 MiB of HBM per device.

v0:
```python
import jax
import jax.numpy as jnp
from jax import lax
from jax.sharding import PartitionSpec as P

HEADS = 17


EPSILON = 1e-05
MASKED = -1e30


def shifted(shard, axis, by):
    length = lax.axis_size(axis)
    pairs = [(i, i + by) for i in range(length) if 0 <= i + by < length]
    return lax.ppermute(shard, axis, pairs)


def shortened(shard):
    return jax.tree.map(lambda a: a.astype(jnp.bfloat16) if a.dtype == jnp.float32 else a, shard)


def shifted_2(block, axis, distance):
    devices = range(lax.axis_size(axis))
    route = [((i - distance) % len(devices), i) for i in devices]
    return lax.ppermute(block, axis, route)


def layer_norm(values, gain_row, shift_row):
    centre = values - jnp.mean(values, axis=-1, keepdims=True)
    spread = jnp.mean(centre * centre, axis=-1, keepdims=True)
    return centre * lax.rsqrt(spread + EPSILON) * gain_row + shift_row


def block_mask(source, cycle_place, seq_rows):
    row_ids = jnp.arange(seq_rows, dtype=jnp.int32)
    diagonal = row_ids[:, None] >= row_ids[None, :]
    return jnp.where(source == cycle_place, diagonal, source < cycle_place)


def cycle_forward(queries, key_rows, value_rows, cycle_place, cycle_size, score_scale):
    seq_rows, head_count, head_size = queries.shape
    run_peak = jnp.full((head_count, seq_rows), MASKED, jnp.float32)
    run_total = jnp.zeros((head_count, seq_rows), jnp.float32)
    run_sum = jnp.zeros((seq_rows, head_count, head_size), jnp.float32)
    state = (run_peak, run_total, run_sum)
    kv_block = jnp.stack((key_rows, value_rows))
    for turn_index in range(cycle_size):
        source = cycle_place - turn_index
        allowed = block_mask(source, cycle_place, seq_rows)

        def update(carry, kv_now=kv_block, allowed_now=allowed):
            old_peak, old_total, old_sum = carry
            scores = (
                jnp.einsum("qhd,khd->hqk", queries, kv_now[0], preferred_element_type=jnp.float32)
                * score_scale
            )
            scores = jnp.where(allowed_now[None], scores, MASKED)
            new_peak = jnp.maximum(old_peak, jnp.max(scores, axis=-1))
            correction = jnp.exp(old_peak - new_peak)
            exp_scores = jnp.exp(scores - new_peak[:, :, None])
            new_total = old_total * correction + jnp.sum(exp_scores, axis=-1)
            new_sum = old_sum * correction.T[:, :, None] + jnp.einsum(
                "hqk,khd->qhd",
                exp_scores.astype(jnp.bfloat16),
                kv_now[1],
                preferred_element_type=jnp.float32,
            )
            return (new_peak, new_total, new_sum)

        def unchanged(carry):
            return carry

        state = lax.cond(source >= 0, update, unchanged, state)
        if turn_index < cycle_size - 1:
            kv_block = shifted(kv_block, "ctx", 1)
    run_peak, run_total, run_sum = state
    attended = run_sum / run_total.T[:, :, None]
    return (attended, run_peak + jnp.log(run_total))


def cycle_backward(
    queries,
    key_rows,
    value_rows,
    grad_attended,
    log_total,
    row_delta,
    cycle_place,
    cycle_size,
    score_scale,
):
    seq_rows, head_count, head_size = queries.shape
    kv_block = jnp.stack((key_rows, value_rows))
    kv_grads = jnp.zeros((2, seq_rows, head_count, head_size), jnp.float32)
    grad_queries = jnp.zeros((seq_rows, head_count, head_size), jnp.float32)
    for turn_index in range(cycle_size):
        source = cycle_place - turn_index
        allowed = block_mask(source, cycle_place, seq_rows)

        def update(carry, kv_now=kv_block, allowed_now=allowed):
            scores = (
                jnp.einsum("qhd,khd->hqk", queries, kv_now[0], preferred_element_type=jnp.float32)
                * score_scale
            )
            scores = jnp.where(allowed_now[None], scores, MASKED)
            probs = jnp.exp(scores - log_total[:, :, None])
            value_part = jnp.einsum(
                "hqk,qhd->khd",
                probs.astype(jnp.bfloat16),
                grad_attended,
                preferred_element_type=jnp.float32,
            )
            grad_probs = jnp.einsum(
                "qhd,khd->hqk", grad_attended, kv_now[1], preferred_element_type=jnp.float32
            )
            grad_scores = (probs * (grad_probs - row_delta[:, :, None]) * score_scale).astype(
                jnp.bfloat16
            )
            new_queries = carry + jnp.einsum(
                "hqk,khd->qhd", grad_scores, kv_now[0], preferred_element_type=jnp.float32
            )
            key_part = jnp.einsum(
                "hqk,qhd->khd", grad_scores, queries, preferred_element_type=jnp.float32
            )
            return (new_queries, jnp.stack((key_part, value_part)))

        def unchanged(carry):
            return (carry, jnp.zeros((2, seq_rows, head_count, head_size), jnp.float32))

        grad_queries, kv_part = lax.cond(source >= 0, update, unchanged, grad_queries)
        kv_grads = shifted_2(shortened(kv_grads + kv_part), "ctx", 1)
        if turn_index < cycle_size - 1:
            kv_block = shifted(kv_block, "ctx", 1)
    return (grad_queries, kv_grads[0], kv_grads[1])


def column_sum(values):
    return jnp.sum(values.astype(jnp.float32), axis=0)


def on_device(
    layer_input,
    output_grad,
    attn_gain,
    attn_shift,
    merged_weight,
    query_bias,
    value_bias,
    out_weight,
    out_bias,
    mlp_gain,
    mlp_shift,
    up_weight,
    up_bias,
    down_weight,
    down_bias,
):
    micro_count = layer_input.shape[0]
    seq_rows = layer_input.shape[2]
    model_width = layer_input.shape[3]
    head_size = model_width // HEADS
    score_scale = head_size ** (-0.5)
    cycle_size = lax.axis_size("ctx")
    cycle_place = lax.axis_index("ctx")
    outputs = []
    input_grads = []
    share_sums = None
    for micro_index in range(micro_count):
        gathered = (
            lax.all_gather(attn_gain, "fsdp", axis=0, tiled=True),
            lax.all_gather(attn_shift, "fsdp", axis=0, tiled=True),
            lax.all_gather(merged_weight, "fsdp", axis=0, tiled=True),
            lax.all_gather(query_bias, "fsdp", axis=0, tiled=True),
            lax.all_gather(value_bias, "fsdp", axis=0, tiled=True),
            lax.all_gather(out_weight, "fsdp", axis=0, tiled=True),
            lax.all_gather(out_bias, "fsdp", axis=0, tiled=True),
            lax.all_gather(mlp_gain, "fsdp", axis=0, tiled=True),
            lax.all_gather(mlp_shift, "fsdp", axis=0, tiled=True),
            lax.all_gather(up_weight, "fsdp", axis=0, tiled=True),
            lax.all_gather(up_bias, "fsdp", axis=0, tiled=True),
            lax.all_gather(down_weight, "fsdp", axis=0, tiled=True),
            lax.all_gather(down_bias, "fsdp", axis=0, tiled=True),
        )
        (
            gain_one,
            shift_one,
            merged_full,
            qbias_full,
            vbias_full,
            outw_full,
            outb_full,
            gain_two,
            shift_two,
            upw_full,
            upb_full,
            downw_full,
            downb_full,
        ) = gathered
        values = layer_input[micro_index, 0].astype(jnp.float32)
        gain_one_f = gain_one.astype(jnp.float32)
        shift_one_f = shift_one.astype(jnp.float32)
        gain_two_f = gain_two.astype(jnp.float32)
        shift_two_f = shift_two.astype(jnp.float32)
        normed = layer_norm(values, gain_one_f, shift_one_f).astype(jnp.bfloat16)
        merged_rows = jnp.dot(normed, merged_full, preferred_element_type=jnp.float32)
        queries = (merged_rows[:, :model_width] + qbias_full.astype(jnp.float32)).astype(
            jnp.bfloat16
        )
        key_rows = merged_rows[:, model_width : 2 * model_width].astype(jnp.bfloat16)
        value_rows = (merged_rows[:, 2 * model_width :] + vbias_full.astype(jnp.float32)).astype(
            jnp.bfloat16
        )
        queries = queries.reshape(seq_rows, HEADS, head_size)
        key_rows = key_rows.reshape(seq_rows, HEADS, head_size)
        value_rows = value_rows.reshape(seq_rows, HEADS, head_size)
        attended_full, log_total = cycle_forward(
            queries, key_rows, value_rows, cycle_place, cycle_size, score_scale
        )
        attended = attended_full.reshape(seq_rows, model_width).astype(jnp.bfloat16)
        middle = (
            values
            + jnp.dot(attended, outw_full, preferred_element_type=jnp.float32)
            + outb_full.astype(jnp.float32)
        )
        normed_two = layer_norm(middle, gain_two_f, shift_two_f).astype(jnp.bfloat16)
        pre_act = jnp.dot(
            normed_two, upw_full, preferred_element_type=jnp.float32
        ) + upb_full.astype(jnp.float32)
        hidden = jax.nn.gelu(pre_act, approximate=False).astype(jnp.bfloat16)
        result = (
            middle
            + jnp.dot(hidden, downw_full, preferred_element_type=jnp.float32)
            + downb_full.astype(jnp.float32)
        )
        outputs.append(result.astype(jnp.bfloat16))
        gathered = (
            lax.all_gather(attn_gain, "fsdp", axis=0, tiled=True),
            lax.all_gather(attn_shift, "fsdp", axis=0, tiled=True),
            lax.all_gather(merged_weight, "fsdp", axis=0, tiled=True),
            lax.all_gather(query_bias, "fsdp", axis=0, tiled=True),
            lax.all_gather(value_bias, "fsdp", axis=0, tiled=True),
            lax.all_gather(out_weight, "fsdp", axis=0, tiled=True),
            lax.all_gather(out_bias, "fsdp", axis=0, tiled=True),
            lax.all_gather(mlp_gain, "fsdp", axis=0, tiled=True),
            lax.all_gather(mlp_shift, "fsdp", axis=0, tiled=True),
            lax.all_gather(up_weight, "fsdp", axis=0, tiled=True),
            lax.all_gather(up_bias, "fsdp", axis=0, tiled=True),
            lax.all_gather(down_weight, "fsdp", axis=0, tiled=True),
            lax.all_gather(down_bias, "fsdp", axis=0, tiled=True),
        )
        (
            gain_one,
            shift_one,
            merged_full,
            qbias_full,
            vbias_full,
            outw_full,
            outb_full,
            gain_two,
            shift_two,
            upw_full,
            upb_full,
            downw_full,
            downb_full,
        ) = gathered
        grad_rows = output_grad[micro_index, 0].astype(jnp.float32)
        grad_mlp = grad_rows.astype(jnp.bfloat16)
        grad_downw = jnp.einsum("ti,tj->ij", hidden, grad_mlp, preferred_element_type=jnp.float32)
        grad_downb = column_sum(grad_mlp)
        grad_hidden = jnp.einsum(
            "tj,ij->ti", grad_mlp, downw_full, preferred_element_type=jnp.float32
        )
        unused_out, gelu_back = jax.vjp(
            lambda inner: jax.nn.gelu(inner, approximate=False), pre_act
        )
        grad_pre = gelu_back(grad_hidden)[0].astype(jnp.bfloat16)
        grad_upw = jnp.einsum("ti,tj->ij", normed_two, grad_pre, preferred_element_type=jnp.float32)
        grad_upb = column_sum(grad_pre)
        grad_normed_two = jnp.einsum(
            "tj,ij->ti", grad_pre, upw_full, preferred_element_type=jnp.float32
        )
        unused_two, norm_two_back = jax.vjp(layer_norm, middle, gain_two_f, shift_two_f)
        middle_part, grad_gain_two, grad_shift_two = norm_two_back(grad_normed_two)
        grad_middle = grad_rows + middle_part
        grad_attn = grad_middle.astype(jnp.bfloat16)
        grad_outw = jnp.einsum("ti,tj->ij", attended, grad_attn, preferred_element_type=jnp.float32)
        grad_outb = column_sum(grad_attn)
        grad_attended = jnp.einsum(
            "tj,ij->ti", grad_attn, outw_full, preferred_element_type=jnp.float32
        ).astype(jnp.bfloat16)
        grad_attended = grad_attended.reshape(seq_rows, HEADS, head_size)
        row_delta = jnp.sum(grad_attended.astype(jnp.float32) * attended_full, axis=-1).T
        grad_queries, grad_keys, grad_values = cycle_backward(
            queries,
            key_rows,
            value_rows,
            grad_attended,
            log_total,
            row_delta,
            cycle_place,
            cycle_size,
            score_scale,
        )
        grad_queries = grad_queries.reshape(seq_rows, model_width).astype(jnp.bfloat16)
        grad_keys = grad_keys.reshape(seq_rows, model_width).astype(jnp.bfloat16)
        grad_values = grad_values.reshape(seq_rows, model_width).astype(jnp.bfloat16)
        grad_merged_rows = jnp.concatenate((grad_queries, grad_keys, grad_values), axis=1)
        grad_merged = jnp.einsum(
            "ti,tj->ij", normed, grad_merged_rows, preferred_element_type=jnp.float32
        )
        grad_qbias = column_sum(grad_queries)
        grad_vbias = column_sum(grad_values)
        grad_normed = jnp.einsum(
            "tj,ij->ti", grad_merged_rows, merged_full, preferred_element_type=jnp.float32
        )
        unused_one, norm_one_back = jax.vjp(layer_norm, values, gain_one_f, shift_one_f)
        input_part, grad_gain_one, grad_shift_one = norm_one_back(grad_normed)
        input_grads.append(grad_middle + input_part)
        shares = (
            lax.psum_scatter(
                grad_gain_one.astype(jnp.bfloat16), "fsdp", scatter_dimension=0, tiled=True
            ).astype(jnp.float32),
            lax.psum_scatter(
                grad_shift_one.astype(jnp.bfloat16), "fsdp", scatter_dimension=0, tiled=True
            ).astype(jnp.float32),
            lax.psum_scatter(
                grad_merged.astype(jnp.bfloat16), "fsdp", scatter_dimension=0, tiled=True
            ).astype(jnp.float32),
            lax.psum_scatter(
                grad_qbias.astype(jnp.bfloat16), "fsdp", scatter_dimension=0, tiled=True
            ).astype(jnp.float32),
            lax.psum_scatter(
                grad_vbias.astype(jnp.bfloat16), "fsdp", scatter_dimension=0, tiled=True
            ).astype(jnp.float32),
            lax.psum_scatter(
                grad_outw.astype(jnp.bfloat16), "fsdp", scatter_dimension=0, tiled=True
            ).astype(jnp.float32),
            lax.psum_scatter(
                grad_outb.astype(jnp.bfloat16), "fsdp", scatter_dimension=0, tiled=True
            ).astype(jnp.float32),
            lax.psum_scatter(
                grad_gain_two.astype(jnp.bfloat16), "fsdp", scatter_dimension=0, tiled=True
            ).astype(jnp.float32),
            lax.psum_scatter(
                grad_shift_two.astype(jnp.bfloat16), "fsdp", scatter_dimension=0, tiled=True
            ).astype(jnp.float32),
            lax.psum_scatter(
                grad_upw.astype(jnp.bfloat16), "fsdp", scatter_dimension=0, tiled=True
            ).astype(jnp.float32),
            lax.psum_scatter(
                grad_upb.astype(jnp.bfloat16), "fsdp", scatter_dimension=0, tiled=True
            ).astype(jnp.float32),
            lax.psum_scatter(
                grad_downw.astype(jnp.bfloat16), "fsdp", scatter_dimension=0, tiled=True
            ).astype(jnp.float32),
            lax.psum_scatter(
                grad_downb.astype(jnp.bfloat16), "fsdp", scatter_dimension=0, tiled=True
            ).astype(jnp.float32),
        )
        share_sums = shares if share_sums is None else jax.tree.map(jnp.add, share_sums, shares)
    matrix_parts = (
        lax.psum_scatter(
            share_sums[2].astype(jnp.bfloat16), "ctx", scatter_dimension=1, tiled=True
        ).astype(jnp.float32),
        lax.psum_scatter(
            share_sums[5].astype(jnp.bfloat16), "ctx", scatter_dimension=1, tiled=True
        ).astype(jnp.float32),
        lax.psum_scatter(
            share_sums[9].astype(jnp.bfloat16), "ctx", scatter_dimension=1, tiled=True
        ).astype(jnp.float32),
        lax.psum_scatter(
            share_sums[11].astype(jnp.bfloat16), "ctx", scatter_dimension=1, tiled=True
        ).astype(jnp.float32),
    )
    matrix_sums = (
        lax.all_gather(matrix_parts[0].astype(jnp.bfloat16), "ctx", axis=1, tiled=True).astype(
            jnp.float32
        ),
        lax.all_gather(matrix_parts[1].astype(jnp.bfloat16), "ctx", axis=1, tiled=True).astype(
            jnp.float32
        ),
        lax.all_gather(matrix_parts[2].astype(jnp.bfloat16), "ctx", axis=1, tiled=True).astype(
            jnp.float32
        ),
        lax.all_gather(matrix_parts[3].astype(jnp.bfloat16), "ctx", axis=1, tiled=True).astype(
            jnp.float32
        ),
    )
    vector_sums = lax.psum(
        (
            share_sums[0],
            share_sums[1],
            share_sums[3],
            share_sums[4],
            share_sums[6],
            share_sums[7],
            share_sums[8],
            share_sums[10],
            share_sums[12],
        ),
        "ctx",
    )
    layer_output = jnp.stack(outputs)[:, None]
    input_grad = jnp.stack(input_grads)[:, None]
    return (
        layer_output,
        input_grad,
        vector_sums[0],
        vector_sums[1],
        matrix_sums[0],
        vector_sums[2],
        vector_sums[3],
        matrix_sums[1],
        vector_sums[4],
        vector_sums[5],
        vector_sums[6],
        matrix_sums[2],
        vector_sums[7],
        matrix_sums[3],
        vector_sums[8],
    )


def solution(mesh):
    in_specs = (
        P(None, "fsdp", "ctx", None),
        P(None, "fsdp", "ctx", None),
        P("fsdp"),
        P("fsdp"),
        P("fsdp", None),
        P("fsdp"),
        P("fsdp"),
        P("fsdp", None),
        P("fsdp"),
        P("fsdp"),
        P("fsdp"),
        P("fsdp", None),
        P("fsdp"),
        P("fsdp", None),
        P("fsdp"),
    )
    out_specs = (
        P(None, "fsdp", "ctx", None),
        P(None, "fsdp", "ctx", None),
        P("fsdp"),
        P("fsdp"),
        P("fsdp", None),
        P("fsdp"),
        P("fsdp"),
        P("fsdp", None),
        P("fsdp"),
        P("fsdp"),
        P("fsdp"),
        P("fsdp", None),
        P("fsdp"),
        P("fsdp", None),
        P("fsdp"),
    )
    return jax.shard_map(
        on_device, mesh=mesh, in_specs=in_specs, out_specs=out_specs, check_vma=False
    )
```

profile of v0, /device:TPU:0, one launch (start us, length us, event | category | flops | bytes accessed | tf_op | source)
XLA Modules:
  0.0 1196.3 jit_solution(18442542531703493073)
XLA Ops:
  14.1 31.9 %all-reduce.32 = (bf16[4352]{0:T(1024)(128)(2,1)S(1)}, bf16[1088]{0:T(1024)(128)(2,1)S(1)}, bf16[1088]{0:T(1024)(128)(2,1)S(1)}, bf16[1088]{0:T(1024)(128)(2,1)S...) all-reduce(bf16[4352]{0:T(1024)(128)(2,1)S(1)} %dynamic-update-slic, ...), channel_id=1, replica_groups=mesh['ctx'=4,'fsdp'=8] {'fsdp'}, use_global_device_ids=true, to_apply=%add.7 | all-reduce | flops 11968 | bytes 47872
  47.2 38.9 %all-gather.10.cloned.1.call-done = bf16[1088,3264]{1,0:T(8,128)(2,1)} async-done(((bf16[136,3264]{1,0:T(8,128)(2,1)}), bf16[1088,3264]{1,0:T(8,128)(2,1)}) %all-gather.10.cloned.1.call-update) | async-done | bytes 7102480 | tf_op jit(solution)/shard_map/all_gather | solution.py:173
  86.0 6.8 fusion.405
  93.0 3.7 fusion.402
  102.1 24.1 %collective-permute-done.3 = bf16[2,256,17,64]{1,3,2,0:T(8,128)(2,1)S(1)} collective-permute-done((bf16[2,256,17,64]{1,3,2,0:T(8,128)(2,1)S(1)}, bf16[2,256,17,64]{1,3,2,0:T(8,128)(2,1)S(1)}, u32[]{:S(2)}, u32[]{:S(2)}) %collective-permute-start.3) | collective-permute-done | bytes 1114144 | tf_op jit(solution)/shard_map/ppermute | solution.py:16
  127.3 5.4 collective-permute-start.4
  132.6 22.4 %collective-permute-done.4 = bf16[2,256,17,64]{1,3,2,0:T(8,128)(2,1)} collective-permute-done((bf16[2,256,17,64]{1,3,2,0:T(8,128)(2,1)S(1)}, bf16[2,256,17,64]{1,3,2,0:T(8,128)(2,1)}, u32[]{:S(2)}, u32[]{:S(2)}) %collective-permute-start.4) | collective-permute-done | bytes 1114144 | tf_op jit(solution)/shard_map/ppermute | solution.py:16
  155.1 5.7 collective-permute-start.5
  163.4 6.9 conditional.20
  170.4 12.0 %collective-permute-done.5 = bf16[2,256,17,64]{1,3,2,0:T(8,128)(2,1)} collective-permute-done((bf16[2,256,17,64]{1,3,2,0:T(8,128)(2,1)}, bf16[2,256,17,64]{1,3,2,0:T(8,128)(2,1)}, u32[]{:S(2)}, u32[]{:S(2)}) %collective-permute-start.5) | collective-permute-done | bytes 1114144 | tf_op jit(solution)/shard_map/ppermute | solution.py:16
  187.4 23.6 %all-gather.14.cloned.1.call-done = bf16[1088,4352]{1,0:T(8,128)(2,1)} async-done(((bf16[136,4352]{1,0:T(8,128)(2,1)}), bf16[1088,4352]{1,0:T(8,128)(2,1)}) %all-gather.14.cloned.1.call-update) | async-done | bytes 9469968 | tf_op jit(solution)/shard_map/all_gather | solution.py:180
  211.0 17.6 %multiply_convert_fusion.8 = (bf16[256,4352]{1,0:T(8,128)(2,1)S(1)}, f32[256,4352]{1,0:T(8,128)}, f32[256,4352]{1,0:T(8,128)}) fusion(f32[4352]{0:T(1024)S(1)} %copy-done.62, bf16[1088,4352]{1,0:T(8,128)(2,1)} %all-gather.14.cloned.1.call-done, f32[256,1088]{0,1:T(8,128)} %copy-done.10, f32[256]{0:T(256)S(1)} %fusion.396, ...), kind=kOutput, calls=%fused_computation.344 | convolution fusion | flops 2499231744 | bytes 21753344 | tf_op jit(solution)/shard_map/dot_general | solution.py:227
  229.9 5.6 convolution_convert_fusion
  238.9 3.5 collective-permute-start
  242.4 24.2 %collective-permute-done = bf16[2,256,17,64]{1,3,2,0:T(8,128)(2,1)S(1)} collective-permute-done((bf16[2,256,17,64]{1,3,2,0:T(8,128)(2,1)S(1)}, bf16[2,256,17,64]{1,3,2,0:T(8,128)(2,1)S(1)}, u32[]{:S(2)}, u32[]{:S(2)}) %collective-permute-start) | collective-permute-done | bytes 1114144 | tf_op jit(solution)/shard_map/ppermute | solution.py:16
  267.5 5.4 collective-permute-start.1
  272.9 22.5 %collective-permute-done.1 = bf16[2,256,17,64]{1,3,2,0:T(8,128)(2,1)} collective-permute-done((bf16[2,256,17,64]{1,3,2,0:T(8,128)(2,1)S(1)}, bf16[2,256,17,64]{1,3,2,0:T(8,128)(2,1)}, u32[]{:S(2)}, u32[]{:S(2)}) %collective-permute-start.1) | collective-permute-done | bytes 1114144 | tf_op jit(solution)/shard_map/ppermute | solution.py:16
  295.4 5.6 collective-permute-start.2
  301.1 7.9 conditional.16
  309.8 13.0 %collective-permute-done.2 = bf16[2,256,17,64]{1,3,2,0:T(8,128)(2,1)} collective-permute-done((bf16[2,256,17,64]{1,3,2,0:T(8,128)(2,1)}, bf16[2,256,17,64]{1,3,2,0:T(8,128)(2,1)}, u32[]{:S(2)}, u32[]{:S(2)}) %collective-permute-start.2) | collective-permute-done | bytes 1114144 | tf_op jit(solution)/shard_map/ppermute | solution.py:16
  326.7 17.6 %multiply_convert_fusion.9 = (bf16[256,4352]{1,0:T(8,128)(2,1)S(1)}, f32[256,4352]{1,0:T(8,128)}, f32[256,4352]{1,0:T(8,128)}) fusion(f32[4352]{0:T(1024)S(1)} %copy-done.63, bf16[1088,4352]{1,0:T(8,128)(2,1)} %all-gather.14.cloned.1.call-done, f32[256,1088]{0,1:T(8,128)S(1)} %get-tuple-element.821, f32[1088]{0:T(1024)S(1)} %convert_element_type.477, ...), kind=kOutput, calls=%fused_computation.357 | convolution fusion | flops 2499231744 | bytes 21753344 | tf_op jit(solution)/shard_map/dot_general | solution.py:227
  345.6 5.7 convolution_convert_fusion.1
  351.9 11.9 fusion.420
  365.1 5.5 convolution_convert_fusion.2
  370.7 12.0 %fusion.421 = (bf16[4352]{0:T(1024)(128)(2,1)}, bf16[256,4352]{1,0:T(8,128)(2,1)S(1)}) fusion(f32[256,4352]{1,0:T(8,128)} %get-tuple-element.763, f32[256,4352]{1,0:T(8,128)} %get-tuple-element.822, bf16[4352,1088]{1,0:T(8,128)(2,1)} %all-gather.16.cloned.1.call-done, bf16[2,1,256,1088]{2,3,1,0:T(8,128)(2,1)S(1)} %copy-done.4), kind=kOutput, calls=%fused_computation.534 | convolution fusion | flops 2441015040 | bytes 21176832 | tf_op jit(solution)/shard_map/tj,ij->ti/dot_general | solution.py:271
  384.0 5.5 convolution_convert_fusion.3
  389.8 6.2 fusion.424
  396.0 7.5 multiply_reduce_fusion.1
  410.6 3.7 convolution_convert_fusion.8
  415.6 8.5 conditional.28
  427.3 3.6 convolution_convert_fusion.9
  432.7 10.7 conditional.24
  443.4 4.0 collective-permute-start.6
  449.6 11.9 collective-permute-done.10
  464.8 11.6 collective-permute-start.11
  476.4 9.0 collective-permute-done.6
  492.7 16.6 %collective-permute-done.11 = bf16[2,256,17,64]{1,3,2,0:T(8,128)(2,1)} collective-permute-done((bf16[2,256,17,64]{1,3,2,0:T(8,128)(2,1)}, bf16[2,256,17,64]{1,3,2,0:T(8,128)(2,1)}, u32[]{:S(2)}, u32[]{:S(2)}) %collective-permute-start.11) | collective-permute-done | bytes 1114144 | tf_op jit(solution)/shard_map/ppermute | solution.py:26
  512.6 20.6 %collective-permute-done.7 = bf16[2,256,17,64]{1,3,2,0:T(8,128)(2,1)} collective-permute-done((bf16[2,256,17,64]{1,3,2,0:T(8,128)(2,1)}, bf16[2,256,17,64]{1,3,2,0:T(8,128)(2,1)}, u32[]{:S(2)}, u32[]{:S(2)}) %collective-permute-start.7) | collective-permute-done | bytes 1114144 | tf_op jit(solution)/shard_map/ppermute | solution.py:26
  537.9 19.1 %collective-permute-done.12 = bf16[2,256,17,64]{1,3,2,0:T(8,128)(2,1)} collective-permute-done((bf16[2,256,17,64]{1,3,2,0:T(8,128)(2,1)}, bf16[2,256,17,64]{1,3,2,0:T(8,128)(2,1)}, u32[]{:S(2)}, u32[]{:S(2)}) %collective-permute-start.12) | collective-permute-done | bytes 1114144 | tf_op jit(solution)/shard_map/ppermute | solution.py:26
  559.4 21.4 %collective-permute-done.8 = bf16[2,256,17,64]{1,3,2,0:T(8,128)(2,1)} collective-permute-done((bf16[2,256,17,64]{1,3,2,0:T(8,128)(2,1)}, bf16[2,256,17,64]{1,3,2,0:T(8,128)(2,1)}, u32[]{:S(2)}, u32[]{:S(2)}) %collective-permute-start.8) | collective-permute-done | bytes 1114144 | tf_op jit(solution)/shard_map/ppermute | solution.py:26
  582.9 21.7 %collective-permute-done.13 = bf16[2,256,17,64]{1,3,2,0:T(8,128)(2,1)S(1)} collective-permute-done((bf16[2,256,17,64]{1,3,2,0:T(8,128)(2,1)S(1)}, bf16[2,256,17,64]{1,3,2,0:T(8,128)(2,1)S(1)}, u32[]{:S(2)}, u32[]{:S(2)}) %collective-permute-start.13) | collective-permute-done | bytes 1114144 | tf_op jit(solution)/shard_map/ppermute | solution.py:26
  604.6 21.3 %collective-permute-done.9 = bf16[2,256,17,64]{1,3,2,0:T(8,128)(2,1)S(1)} collective-permute-done((bf16[2,256,17,64]{1,3,2,0:T(8,128)(2,1)S(1)}, bf16[2,256,17,64]{1,3,2,0:T(8,128)(2,1)S(1)}, u32[]{:S(2)}, u32[]{:S(2)}) %collective-permute-start.9) | collective-permute-done | bytes 1114144 | tf_op jit(solution)/shard_map/ppermute | solution.py:26
  627.3 4.7 convolution_convert_fusion.4
  633.1 4.6 convolution_convert_fusion.5
  643.8 75.7 %reduce-scatter.27.cloned.1.call-done = bf16[136,4352]{1,0:T(8,128)(2,1)} async-done(((bf16[1088,4352]{1,0:T(8,128)(2,1)}), bf16[136,4352]{1,0:T(8,128)(2,1)}) %reduce-scatter.27.cloned.1.call-update) | async-done | bytes 1183760 | tf_op jit(solution)/shard_map/reduce_scatter | solution.py:348
  722.4 3.7 copy.104
  727.1 5.5 fusion.370
  732.7 6.8 fusion.361
  739.5 19.5 %reduce-scatter.43.cloned.1.call-done = bf16[136,1088]{1,0:T(8,128)(2,1)} async-done(((bf16[1088,1088]{1,0:T(8,128)(2,1)}), bf16[136,1088]{1,0:T(8,128)(2,1)}) %reduce-scatter.43.cloned.1.call-update) | async-done | bytes 295952
  759.1 39.5 %reduce-scatter.41.cloned.1.call-done = bf16[136,1088]{1,0:T(8,128)(2,1)} async-done(((bf16[1088,1088]{1,0:T(8,128)(2,1)}), bf16[136,1088]{1,0:T(8,128)(2,1)}) %reduce-scatter.41.cloned.1.call-update) | async-done | bytes 295952
  800.8 78.2 %reduce-scatter.25.cloned.1.call-done = bf16[136,3264]{1,0:T(8,128)(2,1)} async-done(((bf16[1088,3264]{1,0:T(8,128)(2,1)}), bf16[136,3264]{1,0:T(8,128)(2,1)}) %reduce-scatter.25.cloned.1.call-update) | async-done | bytes 887824 | tf_op jit(solution)/shard_map/reduce_scatter | solution.py:327
  879.1 79.7 %reduce-scatter.23.cloned.1.call-done = bf16[136,3264]{1,0:T(8,128)(2,1)} async-done(((bf16[1088,3264]{1,0:T(8,128)(2,1)}), bf16[136,3264]{1,0:T(8,128)(2,1)}) %reduce-scatter.23.cloned.1.call-update) | async-done | bytes 887824 | tf_op jit(solution)/shard_map/reduce_scatter | solution.py:327
  967.2 27.1 %all-reduce.31 = (bf16[1088]{0:T(1024)(128)(2,1)S(1)}, bf16[1088]{0:T(1024)(128)(2,1)S(1)}, bf16[1088]{0:T(1024)(128)(2,1)S(1)}, bf16[1088]{0:T(1024)(128)(2,1)S...) all-reduce(bf16[1088]{0:T(1024)(128)(2,1)S(1)} %dynamic-update-slic, ...), channel_id=1, replica_groups=mesh['ctx'=4,'fsdp'=8] {'fsdp'}, use_global_device_ids=true, to_apply=%add.8 | all-reduce | flops 27200 | bytes 108800
  995.1 16.6 %all-reduce.30 = (f32[136]{0:T(256)}, f32[136]{0:T(256)}, f32[136]{0:T(256)}, f32[136]{0:T(256)}, f32[136]{0:T(256)}, /*index=5*/f32[136]{0:T(256)}, f32[136]{0:T(256)}, f32[544]{0:T(1024)}, f32[136]{0:T(256)}) all-reduce(f32[136]{0:T(256)S(1)} %convert_add_fusion.8, ...), channel_id=1, replica_groups=mesh['ctx'=4,'fsdp'=8] {'ctx'}, use_global_device_ids=true, to_apply=%region_70.71 | all-reduce | flops 1632 | bytes 13056 | tf_op jit(solution)/shard_map/psum | solution.py:390
  1011.7 4.7 all-reduce.35.cloned.1.call-done
  1018.8 8.8 fusion.339
  1027.7 7.9 fusion.338
  1035.6 21.1 %reduce-scatter.39.cloned.1.call-done = bf16[1088,136]{1,0:T(8,128)(2,1)} async-done(((bf16[4352,136]{1,0:T(8,128)(2,1)}), bf16[1088,136]{1,0:T(8,128)(2,1)}) %reduce-scatter.39.cloned.1.call-update) | async-done | bytes 295952
  1064.4 20.8 %reduce-scatter.37.cloned.1.call-done = bf16[272,136]{1,0:T(8,128)(2,1)} async-done(((bf16[1088,136]{1,0:T(8,128)(2,1)}), bf16[272,136]{1,0:T(8,128)(2,1)}) %reduce-scatter.37.cloned.1.call-update) | async-done | bytes 74000
  1086.2 9.6 all-gather.1
  1097.2 23.2 %reduce-scatter.35.cloned.1.call-done = bf16[816,136]{1,0:T(8,128)(2,1)} async-done(((bf16[3264,136]{1,0:T(8,128)(2,1)}), bf16[816,136]{1,0:T(8,128)(2,1)}) %reduce-scatter.35.cloned.1.call-update) | async-done | bytes 221968
  1121.5 16.6 %all-gather = bf16[4,816,136]{1,2,0:T(8,128)(2,1)S(1)} all-gather(bf16[1,816,136]{1,2,0:T(8,128)(2,1)S(1)} %bitcast.544), channel_id=1, replica_groups=mesh['ctx'=4,'fsdp'=8] {'ctx'}, dimensions={0}, use_global_device_ids=true | all-gather | bytes 1109760 | tf_op jit(solution)/shard_map/all_gather | solution.py:377
  1140.8 13.1 %all-gather.18.cloned.1.call-done = bf16[544,1088]{0,1:T(8,128)(2,1)} async-done(((bf16[544,272]{0,1:T(8,128)(2,1)}), bf16[544,1088]{0,1:T(8,128)(2,1)}) %all-gather.18.cloned.1.call-update) | async-done | bytes 1183760 | tf_op jit(solution)/shard_map/all_gather | solution.py:386
  1156.7 27.8 %all-gather.20.cloned.1.call-done = bf16[4,1088,136]{1,2,0:T(8,128)(2,1)} async-done(((bf16[1,1088,136]{1,2,0:T(8,128)(2,1)}), bf16[4,1088,136]{1,2,0:T(8,128)(2,1)}) %all-gather.20.cloned.1.call-update) | async-done | bytes 1183760 | tf_op jit(solution)/shard_map/all_gather | solution.py:383
  (401 shorter events, 155.3 us)
Async XLA Ops:
  7.3 38.8 %copy-start.6 = (bf16[2,1,256,1088]{2,3,1,0:T(8,128)(2,1)S(1)}, bf16[2,1,256,1088]{2,3,1,0:T(8,128)(2,1)}, u32[]{:S(2)}) copy-start(bf16[2,1,256,1088]{2,3,1,0:T(8,128)(2,1)} %param.47) | copy-start | bytes 3342340
  7.3 78.7 %all-gather.10.cloned.1.call-start = ((), (), s32[]{:S(2)}) async-start(), calls=%async_computation.11 | async-start | bytes 8146944 | tf_op jit(solution)/shard_map/all_gather | solution.py:173
  8.0 174.9 %all-gather.12.cloned.1.call-start = ((), (), s32[]{:S(2)}) async-start(), calls=%async_computation.12 | async-start | bytes 2820096 | tf_op jit(solution)/shard_map/all_gather | solution.py:176
  8.8 202.2 %all-gather.14.cloned.1.call-start = ((), (), s32[]{:S(2)}) async-start(), calls=%async_computation.13 | async-start | bytes 10653696 | tf_op jit(solution)/shard_map/all_gather | solution.py:180
  9.5 342.3 %all-gather.16.cloned.1.call-start = ((), (), s32[]{:S(2)}) async-start(), calls=%async_computation.14 | async-start | bytes 11280384 | tf_op jit(solution)/shard_map/all_gather | solution.py:182
  10.1 630.6 %reduce-scatter.33.cloned.1.call-start = ((), (), s32[]{:S(2)}) async-start(), calls=%async_computation.20 | async-start | bytes 11280384 | tf_op jit(solution)/shard_map/reduce_scatter | solution.py:354
  46.0 47.0 %copy-start.84 = (f32[1088]{0:T(1024)}, f32[1088]{0:T(1024)S(1)}, u32[]{:S(2)}) copy-start(f32[1088]{0:T(1024)S(1)} %convert_element_type.467) | copy-start | bytes 13060
  46.0 47.0 %copy-start.60 = (f32[1088]{0:T(1024)}, f32[1088]{0:T(1024)S(1)}, u32[]{:S(2)}) copy-start(f32[1088]{0:T(1024)S(1)} %convert_element_type.466) | copy-start | bytes 13060
  46.2 46.7 %copy-start.64 = (f32[256]{0:T(256)}, f32[256]{0:T(256)S(1)}, u32[]{:S(2)}) copy-start(f32[256]{0:T(256)S(1)} %broadcast_multiply_fusion.3) | copy-start | bytes 3076
  46.3 46.6 %copy-start.66 = (f32[256]{0:T(256)}, f32[256]{0:T(256)S(1)}, u32[]{:S(2)}) copy-start(f32[256]{0:T(256)S(1)} %broadcast_multiply_fusion.1) | copy-start | bytes 3076
  46.6 46.3 %copy-start.74 = (f32[256]{0:T(256)}, f32[256]{0:T(256)S(1)}, u32[]{:S(2)}) copy-start(f32[256]{0:T(256)S(1)} %get-tuple-element.706) | copy-start | bytes 3076
  47.2 45.7 %copy-start.70 = (f32[256]{0:T(256)}, f32[256]{0:T(256)S(1)}, u32[]{:S(2)}) copy-start(f32[256]{0:T(256)S(1)} %fusion.395) | copy-start | bytes 3076
  47.2 45.8 %copy-start.72 = (f32[256]{0:T(256)}, f32[256]{0:T(256)S(1)}, u32[]{:S(2)}) copy-start(f32[256]{0:T(256)S(1)} %fusion.393) | copy-start | bytes 3076
  86.0 7.0 copy-start.92
  93.0 70.4 %copy-start.8 = (bf16[256,1088]{0,1:T(8,128)(2,1)}, bf16[256,1088]{0,1:T(8,128)(2,1)S(1)}, u32[]{:S(2)}) copy-start(bf16[256,1088]{0,1:T(8,128)(2,1)S(1)} %slice.328) | copy-start | bytes 1671172
  98.6 56.5 %copy-start.35 = (bf16[256,1088]{0,1:T(8,128)(2,1)}, bf16[256,1088]{0,1:T(8,128)(2,1)S(1)}, u32[]{:S(2)}) copy-start(bf16[256,1088]{0,1:T(8,128)(2,1)S(1)} %get-tuple-element.796) | copy-start | bytes 1671172
  98.6 83.8 %copy-start = (bf16[256,1088]{0,1:T(8,128)(2,1)}, bf16[256,1088]{0,1:T(8,128)(2,1)S(1)}, u32[]{:S(2)}) copy-start(bf16[256,1088]{0,1:T(8,128)(2,1)S(1)} %get-tuple-element.797) | copy-start | bytes 1671172
  98.7 27.6 %collective-permute-start.3 = (bf16[2,256,17,64]{1,3,2,0:T(8,128)(2,1)S(1)}, bf16[2,256,17,64]{1,3,2,0:T(8,128)(2,1)S(1)}, u32[]{:S(2)}, u32[]{:S(2)}) collective-permute-start(bf16[2,256,17,64]{1,3,2,0:T(8,128)(2,1)S(1)} %pad_maximum_fusion.11), channel_id=1, source_target_pairs={{0,8},{8,16},{16,24},{1,9},{9,17},{17,25},{2,10},{10,18},{18,26},{... | collective-permute-start | bytes 3342344 | tf_op jit(solution)/shard_map/ppermute | solution.py:16
  127.3 27.8 %collective-permute-start.4 = (bf16[2,256,17,64]{1,3,2,0:T(8,128)(2,1)S(1)}, bf16[2,256,17,64]{1,3,2,0:T(8,128)(2,1)}, u32[]{:S(2)}, u32[]{:S(2)}) collective-permute-start(bf16[2,256,17,64]{1,3,2,0:T(8,128)(2,1)S(1)} %collective-permute-done.3), channel_id=1, source_target_pairs={{0,8},{8,16},{16,24},{1,9},{9,17},{17,25},{2,10},{10,18},{18,26},{... | collective-permute-start | bytes 3342344 | tf_op jit(solution)/shard_map/ppermute | solution.py:16
  155.1 27.3 %collective-permute-start.5 = (bf16[2,256,17,64]{1,3,2,0:T(8,128)(2,1)}, bf16[2,256,17,64]{1,3,2,0:T(8,128)(2,1)}, u32[]{:S(2)}, u32[]{:S(2)}) collective-permute-start(bf16[2,256,17,64]{1,3,2,0:T(8,128)(2,1)} %collective-permute-done.4), channel_id=1, source_target_pairs={{0,8},{8,16},{16,24},{1,9},{9,17},{17,25},{2,10},{10,18},{18,26},{... | collective-permute-start | bytes 3342344 | tf_op jit(solution)/shard_map/ppermute | solution.py:16
  163.4 159.4 %copy-start.49 = (pred[256,256]{1,0:T(8,128)(4,1)}, pred[256,256]{1,0:T(8,128)(4,1)S(1)}, u32[]{:S(2)}) copy-start(pred[256,256]{1,0:T(8,128)(4,1)S(1)} %fusion.388) | copy-start | bytes 196612
  182.9 28.0 %copy-start.62 = (f32[4352]{0:T(1024)S(1)}, f32[4352]{0:T(1024)}, u32[]{:S(2)}) copy-start(f32[4352]{0:T(1024)} %convert_element_type.479) | copy-start | bytes 52228
  187.4 41.2 %copy-start.78 = (f32[256]{0:T(256)}, f32[256]{0:T(256)S(1)}, u32[]{:S(2)}) copy-start(f32[256]{0:T(256)S(1)} %multiply_reduce_fusion.6) | copy-start | bytes 3076
  187.4 42.5 %copy-start.4 = (bf16[2,1,256,1088]{2,3,1,0:T(8,128)(2,1)S(1)}, bf16[2,1,256,1088]{2,3,1,0:T(8,128)(2,1)}, u32[]{:S(2)}) copy-start(bf16[2,1,256,1088]{2,3,1,0:T(8,128)(2,1)} %param.48) | copy-start | bytes 3342340
  235.5 405.2 %reduce-scatter.31.cloned.1.call-start = ((), (), s32[]{:S(2)}) async-start(), calls=%async_computation.19 | async-start | bytes 11280384 | tf_op jit(solution)/shard_map/reduce_scatter | solution.py:354
  238.9 27.6 %collective-permute-start = (bf16[2,256,17,64]{1,3,2,0:T(8,128)(2,1)S(1)}, bf16[2,256,17,64]{1,3,2,0:T(8,128)(2,1)S(1)}, u32[]{:S(2)}, u32[]{:S(2)}) collective-permute-start(bf16[2,256,17,64]{1,3,2,0:T(8,128)(2,1)S(1)} %pad_maximum_fusion.10), channel_id=1, source_target_pairs={{0,8},{8,16},{16,24},{1,9},{9,17},{17,25},{2,10},{10,18},{18,26},{... | collective-permute-start | bytes 3342344 | tf_op jit(solution)/shard_map/ppermute | solution.py:16
  267.5 27.9 %collective-permute-start.1 = (bf16[2,256,17,64]{1,3,2,0:T(8,128)(2,1)S(1)}, bf16[2,256,17,64]{1,3,2,0:T(8,128)(2,1)}, u32[]{:S(2)}, u32[]{:S(2)}) collective-permute-start(bf16[2,256,17,64]{1,3,2,0:T(8,128)(2,1)S(1)} %collective-permute-done), channel_id=1, source_target_pairs={{0,8},{8,16},{16,24},{1,9},{9,17},{17,25},{2,10},{10,18},{18,26},{... | collective-permute-start | bytes 3342344 | tf_op jit(solution)/shard_map/ppermute | solution.py:16
  295.4 27.4 %collective-permute-start.2 = (bf16[2,256,17,64]{1,3,2,0:T(8,128)(2,1)}, bf16[2,256,17,64]{1,3,2,0:T(8,128)(2,1)}, u32[]{:S(2)}, u32[]{:S(2)}) collective-permute-start(bf16[2,256,17,64]{1,3,2,0:T(8,128)(2,1)} %collective-permute-done.1), channel_id=1, source_target_pairs={{0,8},{8,16},{16,24},{1,9},{9,17},{17,25},{2,10},{10,18},{18,26},{... | collective-permute-start | bytes 3342344 | tf_op jit(solution)/shard_map/ppermute | solution.py:16
  326.5 17.8 %copy-start.13 = (f32[256,1088]{0,1:T(8,128)}, f32[256,1088]{0,1:T(8,128)S(1)}, u32[]{:S(2)}) copy-start(f32[256,1088]{0,1:T(8,128)S(1)} %get-tuple-element.821) | copy-start | bytes 3342340
  351.4 292.4 %reduce-scatter.29.cloned.1.call-start = ((), (), s32[]{:S(2)}) async-start(), calls=%async_computation.18 | async-start | bytes 10653696 | tf_op jit(solution)/shard_map/reduce_scatter | solution.py:348
  351.8 13.3 %copy-start.11 = (f32[256,1088]{0,1:T(8,128)S(1)}, f32[256,1088]{0,1:T(8,128)}, u32[]{:S(2)}) copy-start(f32[256,1088]{0,1:T(8,128)} %copy-done.10) | copy-start | bytes 3342340
  370.6 348.8 %reduce-scatter.27.cloned.1.call-start = ((), (), s32[]{:S(2)}) async-start(), calls=%async_computation.17 | async-start | bytes 10653696 | tf_op jit(solution)/shard_map/reduce_scatter | solution.py:348
  370.7 13.4 %copy-start.14 = (f32[256,1088]{0,1:T(8,128)S(1)}, f32[256,1088]{0,1:T(8,128)}, u32[]{:S(2)}) copy-start(f32[256,1088]{0,1:T(8,128)} %copy-done.13) | copy-start | bytes 3342340
  389.5 369.5 %reduce-scatter.43.cloned.1.call-start = ((), (), s32[]{:S(2)}) async-start(), calls=%async_computation.28 | async-start | bytes 2820096
  396.0 7.5 copy-start.79
  408.9 389.6 %reduce-scatter.41.cloned.1.call-start = ((), (), s32[]{:S(2)}) async-start(), calls=%async_computation.27 | async-start | bytes 2820096
  424.1 37.4 %collective-permute-start.10 = (bf16[2,256,17,64]{1,3,2,0:T(8,128)(2,1)}, bf16[2,256,17,64]{1,3,2,0:T(8,128)(2,1)}, u32[]{:S(2)}, u32[]{:S(2)}) collective-permute-start(bf16[2,256,17,64]{1,3,2,0:T(8,128)(2,1)} %get-tuple-element.461), channel_id=1, source_target_pairs={{24,0},{0,8},{8,16},{16,24},{25,1},{1,9},{9,17},{17,25},{26,2},{2,... | collective-permute-start | bytes 3342344 | tf_op jit(solution)/shard_map/ppermute | solution.py:26
  432.7 14.6 %copy-start.53 = (pred[256,256]{1,0:T(8,128)(4,1)S(1)}, pred[256,256]{1,0:T(8,128)(4,1)}, u32[]{:S(2)}) copy-start(pred[256,256]{1,0:T(8,128)(4,1)} %fusion.390) | copy-start | bytes 196612
  443.4 42.0 %collective-permute-start.6 = (bf16[2,256,17,64]{1,3,2,0:T(8,128)(2,1)}, bf16[2,256,17,64]{1,3,2,0:T(8,128)(2,1)}, u32[]{:S(2)}, u32[]{:S(2)}) collective-permute-start(bf16[2,256,17,64]{1,3,2,0:T(8,128)(2,1)} %get-tuple-element.452), channel_id=1, source_target_pairs={{24,0},{0,8},{8,16},{16,24},{25,1},{1,9},{9,17},{17,25},{26,2},{2,... | collective-permute-start | bytes 3342344 | tf_op jit(solution)/shard_map/ppermute | solution.py:26
  464.8 44.5 %collective-permute-start.11 = (bf16[2,256,17,64]{1,3,2,0:T(8,128)(2,1)}, bf16[2,256,17,64]{1,3,2,0:T(8,128)(2,1)}, u32[]{:S(2)}, u32[]{:S(2)}) collective-permute-start(bf16[2,256,17,64]{1,3,2,0:T(8,128)(2,1)} %add_convert_fusion.6), channel_id=1, source_target_pairs={{24,0},{0,8},{8,16},{16,24},{25,1},{1,9},{9,17},{17,25},{26,2},{2,... | collective-permute-start | bytes 3342344 | tf_op jit(solution)/shard_map/ppermute | solution.py:26
  488.1 45.0 %collective-permute-start.7 = (bf16[2,256,17,64]{1,3,2,0:T(8,128)(2,1)}, bf16[2,256,17,64]{1,3,2,0:T(8,128)(2,1)}, u32[]{:S(2)}, u32[]{:S(2)}) collective-permute-start(bf16[2,256,17,64]{1,3,2,0:T(8,128)(2,1)} %add_convert_fusion.9), channel_id=1, source_target_pairs={{24,0},{0,8},{8,16},{16,24},{25,1},{1,9},{9,17},{17,25},{26,2},{2,... | collective-permute-start | bytes 3342344 | tf_op jit(solution)/shard_map/ppermute | solution.py:26
  490.6 388.5 %reduce-scatter.25.cloned.1.call-start = ((), (), s32[]{:S(2)}) async-start(), calls=%async_computation.16 | async-start | bytes 8146944 | tf_op jit(solution)/shard_map/reduce_scatter | solution.py:327
  512.6 44.4 %collective-permute-start.12 = (bf16[2,256,17,64]{1,3,2,0:T(8,128)(2,1)}, bf16[2,256,17,64]{1,3,2,0:T(8,128)(2,1)}, u32[]{:S(2)}, u32[]{:S(2)}) collective-permute-start(bf16[2,256,17,64]{1,3,2,0:T(8,128)(2,1)} %add_convert_fusion.5), channel_id=1, source_target_pairs={{24,0},{0,8},{8,16},{16,24},{25,1},{1,9},{9,17},{17,25},{26,2},{2,... | collective-permute-start | bytes 3342344 | tf_op jit(solution)/shard_map/ppermute | solution.py:26
  535.8 45.1 %collective-permute-start.8 = (bf16[2,256,17,64]{1,3,2,0:T(8,128)(2,1)}, bf16[2,256,17,64]{1,3,2,0:T(8,128)(2,1)}, u32[]{:S(2)}, u32[]{:S(2)}) collective-permute-start(bf16[2,256,17,64]{1,3,2,0:T(8,128)(2,1)} %add_convert_fusion.8), channel_id=1, source_target_pairs={{24,0},{0,8},{8,16},{16,24},{25,1},{1,9},{9,17},{17,25},{26,2},{2,... | collective-permute-start | bytes 3342344 | tf_op jit(solution)/shard_map/ppermute | solution.py:26
  559.4 45.3 %collective-permute-start.13 = (bf16[2,256,17,64]{1,3,2,0:T(8,128)(2,1)S(1)}, bf16[2,256,17,64]{1,3,2,0:T(8,128)(2,1)S(1)}, u32[]{:S(2)}, u32[]{:S(2)}) collective-permute-start(bf16[2,256,17,64]{1,3,2,0:T(8,128)(2,1)S(1)} %add_convert_fusion.4), channel_id=1, source_target_pairs={{24,0},{0,8},{8,16},{16,24},{25,1},{1,9},{9,17},{17,25},{26,2},{2,... | collective-permute-start | bytes 3342344 | tf_op jit(solution)/shard_map/ppermute | solution.py:26
  582.5 43.4 %collective-permute-start.9 = (bf16[2,256,17,64]{1,3,2,0:T(8,128)(2,1)S(1)}, bf16[2,256,17,64]{1,3,2,0:T(8,128)(2,1)S(1)}, u32[]{:S(2)}, u32[]{:S(2)}) collective-permute-start(bf16[2,256,17,64]{1,3,2,0:T(8,128)(2,1)S(1)} %add_convert_fusion.7), channel_id=1, source_target_pairs={{24,0},{0,8},{8,16},{16,24},{25,1},{1,9},{9,17},{17,25},{26,2},{2,... | collective-permute-start | bytes 3342344 | tf_op jit(solution)/shard_map/ppermute | solution.py:26
  582.8 43.5 %copy-start.57 = (bf16[256,17,64]{0,2,1:T(8,128)(2,1)}, bf16[256,17,64]{0,2,1:T(8,128)(2,1)S(1)}, u32[]{:S(2)}) copy-start(bf16[256,17,64]{0,2,1:T(8,128)(2,1)S(1)} %get-tuple-element.771) | copy-start | bytes 1671172
  582.8 44.5 %copy-start.7 = (bf16[2,1,256,1088]{2,3,1,0:T(8,128)(2,1)S(1)}, bf16[2,1,256,1088]{2,3,1,0:T(8,128)(2,1)}, u32[]{:S(2)}) copy-start(bf16[2,1,256,1088]{2,3,1,0:T(8,128)(2,1)} %param.47) | copy-start | bytes 3342340
  582.8 44.5 %copy-start.61 = (f32[1088]{0:T(1024)S(1)}, f32[1088]{0:T(1024)}, u32[]{:S(2)}) copy-start(f32[1088]{0:T(1024)} %copy-done.60) | copy-start | bytes 13060
  582.9 44.5 %copy-start.67 = (f32[256]{0:T(256)S(1)}, f32[256]{0:T(256)}, u32[]{:S(2)}) copy-start(f32[256]{0:T(256)} %copy-done.66) | copy-start | bytes 3076
  582.9 44.4 %copy-start.71 = (f32[256]{0:T(256)S(1)}, f32[256]{0:T(256)}, u32[]{:S(2)}) copy-start(f32[256]{0:T(256)} %copy-done.70) | copy-start | bytes 3076
  582.9 44.4 %copy-start.85 = (f32[1088]{0:T(1024)S(1)}, f32[1088]{0:T(1024)}, u32[]{:S(2)}) copy-start(f32[1088]{0:T(1024)} %copy-done.84) | copy-start | bytes 13060
  632.0 326.8 %reduce-scatter.23.cloned.1.call-start = ((), (), s32[]{:S(2)}) async-start(), calls=%async_computation.15 | async-start | bytes 8146944 | tf_op jit(solution)/shard_map/reduce_scatter | solution.py:327
  637.8 378.6 %all-reduce.35.cloned.1.call-start = ((), (), s32[]{:S(2)}) async-start(), calls=%async_computation.26 | async-start | bytes 2506752
  643.7 413.0 %reduce-scatter.39.cloned.1.call-start = ((), (), s32[]{:S(2)}) async-start(), calls=%async_computation.25 | async-start | bytes 2785280
  726.1 359.1 %reduce-scatter.37.cloned.1.call-start = ((), (), s32[]{:S(2)}) async-start(), calls=%async_computation.24 | async-start | bytes 696320
  732.7 6.9 copy-start.22
  800.8 319.6 %reduce-scatter.35.cloned.1.call-start = ((), (), s32[]{:S(2)}) async-start(), calls=%async_computation.23 | async-start | bytes 2088960
  964.0 189.9 %all-gather.18.cloned.1.call-start = ((), (), s32[]{:S(2)}) async-start(), calls=%async_computation.21 | async-start | bytes 1740800 | tf_op jit(solution)/shard_map/all_gather | solution.py:386
  1018.6 165.9 %all-gather.20.cloned.1.call-start = ((), (), s32[]{:S(2)}) async-start(), calls=%async_computation.22 | async-start | bytes 1566720 | tf_op jit(solution)/shard_map/all_gather | solution.py:383
  1018.8 8.9 copy-start.16
  1018.8 8.9 copy-start.31
  1035.6 24.2 %copy-start.81 = (f32[256]{0:T(256)S(1)}, f32[256]{0:T(256)}, u32[]{:S(2)}) copy-start(f32[256]{0:T(256)} %copy-done.80) | copy-start | bytes 3076
  1035.6 24.2 %copy-start.83 = (f32[256]{0:T(256)S(1)}, f32[256]{0:T(256)}, u32[]{:S(2)}) copy-start(f32[256]{0:T(256)} %copy-done.82) | copy-start | bytes 3076
  (66 other events, 203.8 us)
Sparse Core Ops, SparseCore 0:
  9.8 76.2 all-gather.9
  87.7 31.5 all-gather.11
  120.9 90.0 all-gather.13
  212.5 94.0 all-gather.15
  308.7 103.4 reduce-scatter.32
  414.4 103.4 reduce-scatter.30
  520.2 98.4 reduce-scatter.28
  621.0 98.4 reduce-scatter.26
  722.3 36.6 reduce-scatter.42
  761.4 37.1 reduce-scatter.40
  800.9 78.1 reduce-scatter.24
  881.4 77.4 reduce-scatter.22
  962.0 54.3 all-reduce.34
  1020.1 36.5 reduce-scatter.38
  1060.2 24.9 reduce-scatter.36
  1088.7 31.6 reduce-scatter.34
  1122.6 31.1 all-gather.17
  1156.1 28.3 all-gather.19
where the time goes:
time: 1210 us; the launch traced here: 1200 us
  waiting for transfers between devices  728 us (60%)
  matrix products  186 us (15%)
  blocking collectives  102 us (8%)
  other arithmetic  57.6 us (5%)
  local copies, waits for them, and re-layouts  51.9 us (4%)
  starting transfers between devices  49.9 us (4%)
  between operations  19.2 us (2%)
    reduce_scatter x2, waiting for transfers between devices, on_device(): lax.psum_scatter(grad_merged.astype(jnp.bfloat16), 'fsdp', scatter_dimens...  158 us
    ppermute x8, waiting for transfers between devices, shifted_2(): return lax.ppermute(block, axis, route)  142 us
    unnamed x24, waiting for transfers between devices  132 us
    ppermute x6, waiting for transfers between devices, shifted(): return lax.ppermute(shard, axis, pairs)  118 us
    reduce_scatter x2, waiting for transfers between devices, on_device(): lax.psum_scatter(grad_upw.astype(jnp.bfloat16), 'fsdp', scatter_dimension...  75.7 us
    unnamed x2, blocking collectives  59 us
    all_gather x1, waiting for transfers between devices, on_device(): lax.all_gather(merged_weight, 'fsdp', axis=0, tiled=True)  38.9 us
    unnamed x222, local copies, waits for them, and re-layouts  36.3 us
  transfers between devices with their start and end apart: 32, of which 27 were waited for; matrix products, arithmetic and copies ran while one was open for 23% of the time, Pallas kernels for 0%

commit v1 on v0

v1 whole, which is shorter than its diff:
```python
import functools

import jax
import jax.numpy as jnp
from jax import lax
from jax.experimental import pallas as pl
from jax.experimental.pallas import tpu as pltpu
from jax.sharding import PartitionSpec as P

HEADS = 17
EPSILON = 1e-05
MASKED = -1e30
VMEM_BYTES = 56 * 1024 * 1024
BF = jnp.bfloat16
F32 = jnp.float32


def swap(block, bit):
    size = lax.axis_size("ctx")
    return lax.ppermute(block, "ctx", [(i, i ^ bit) for i in range(size)])


def gather_ctx(block):
    size = lax.axis_size("ctx")
    if size != 4:
        return [block] + [swap(block, r) for r in range(1, size)]
    half = block.shape[0] // 2
    one = swap(block, 1)
    two = swap(block, 2)
    top = swap(two[:half], 1)
    bottom = swap(one[half:], 2)
    return [block, one, two, jnp.concatenate((top, bottom))]


def add_f32(a, b):
    return a.astype(F32) + b.astype(F32)


def reduce_ctx(parts):
    size = lax.axis_size("ctx")
    if size != 4:
        total = parts[0].astype(F32)
        for r in range(1, size):
            total = total + swap(parts[r], r).astype(F32)
        return total
    half = parts[0].shape[0] // 2
    from_one = swap(parts[3][:half], 1)
    from_two = swap(parts[3][half:], 2)
    for_two = jnp.concatenate(
        (add_f32(parts[2][:half], from_one).astype(BF), parts[2][half:].astype(BF))
    )
    for_one = jnp.concatenate(
        (parts[1][:half].astype(BF), add_f32(parts[1][half:], from_two).astype(BF))
    )
    got_one = swap(for_one, 1)
    got_two = swap(for_two, 2)
    return parts[0].astype(F32) + got_one.astype(F32) + got_two.astype(F32)


def trade_ctx(parts):
    return [parts[0]] + [swap(parts[r], r) for r in range(1, len(parts))]


def normal(values):
    centre = values - jnp.mean(values, axis=-1, keepdims=True)
    spread = jnp.mean(centre * centre, axis=-1, keepdims=True)
    rate = lax.rsqrt(spread + EPSILON)
    return centre * rate, rate


def norm_back(normed, rate, scaled):
    return rate * (
        scaled
        - jnp.mean(scaled, axis=-1, keepdims=True)
        - normed * jnp.mean(scaled * normed, axis=-1, keepdims=True)
    )


def dot(a, b, dims):
    return lax.dot_general(a, b, ((dims[0], dims[1]), ((), ())), preferred_element_type=F32)


NN = ((1,), (0,))
NT = ((1,), (1,))


def head_lanes(shape, head, head_size):
    lane = lax.broadcasted_iota(jnp.int32, shape, 1)
    return (lane >= head * head_size) & (lane < (head + 1) * head_size)


def attend_kernel(
    blocks, rows, heads, head_size, place, qkv, out, tail_out, log, tail_log, keys, values_t, tail_kv
):
    width = heads * head_size
    me = place[0]
    for j in range(blocks):
        slot = pl.ds(pl.multiple_of((me ^ j) * rows, rows), rows)
        here = pl.ds(j * rows, rows)
        keys[here, :] = qkv[slot, width : 2 * width]
        values_t[:width, here] = qkv[slot, 2 * width : 3 * width].T
        pair = qkv[slot, 3 * width : 3 * width + 2 * head_size]
        tail_kv[here, :] = pair
        values_t[width:, here] = pair.T
    key_row = lax.broadcasted_iota(jnp.int32, (rows, rows), 0)
    query_row = lax.broadcasted_iota(jnp.int32, (rows, rows), 1)

    def softmax_values(scores, value_rows):
        peak = scores[0].max(axis=0, keepdims=True)
        for s in scores[1:]:
            peak = jnp.maximum(peak, s.max(axis=0, keepdims=True))
        total = jnp.zeros((1, rows), F32)
        product = jnp.zeros((head_size, rows), F32)
        for j, s in enumerate(scores):
            e = jnp.exp(s - peak)
            total = total + e.sum(axis=0, keepdims=True)
            product = product + dot(
                values_t[value_rows, j * rows : (j + 1) * rows], e.astype(BF), NN
            )
        return product / total, peak + jnp.log(total)

    for i in range(blocks):
        slot = pl.ds(pl.multiple_of((me ^ i) * rows, rows), rows)
        query = qkv[slot, :width]
        products = []
        for h in range(heads):
            masked = jnp.where(head_lanes((rows, width), h, head_size), query, jnp.zeros_like(query))
            scores = []
            for j in range(i + 1):
                s = dot(keys[j * rows : (j + 1) * rows, :], masked, NT)
                if j == i:
                    s = jnp.where(key_row <= query_row, s, MASKED)
                scores.append(s)
            product, total = softmax_values(scores, pl.ds(h * head_size, head_size))
            products.append(product)
            log[h : h + 1, i * rows : (i + 1) * rows] = total
        out[slot, :] = jnp.concatenate(products, axis=0).T.astype(BF)

    query = qkv[0:rows, 3 * width + 2 * head_size : 3 * width + 3 * head_size]
    scores = []
    for j in range(blocks):
        s = dot(tail_kv[j * rows : (j + 1) * rows, :head_size], query, NT)
        scores.append(jnp.where(j * rows + key_row <= me * rows + query_row, s, MASKED))
    product, total = softmax_values(scores, pl.ds(width + head_size, head_size))
    tail_out[...] = product.T.astype(BF)
    tail_log[...] = total


def attend(place, qkv, blocks, rows, heads, head_size):
    width = heads * head_size
    length = blocks * rows
    return pl.pallas_call(
        functools.partial(attend_kernel, blocks, rows, heads, head_size),
        out_shape=(
            jax.ShapeDtypeStruct((length, width), BF),
            jax.ShapeDtypeStruct((rows, head_size), BF),
            jax.ShapeDtypeStruct((heads, length), F32),
            jax.ShapeDtypeStruct((1, rows), F32),
        ),
        in_specs=[
            pl.BlockSpec(memory_space=pltpu.SMEM),
            pl.BlockSpec(memory_space=pltpu.VMEM),
        ],
        out_specs=(pl.BlockSpec(memory_space=pltpu.VMEM),) * 4,
        scratch_shapes=[
            pltpu.VMEM((length, width), BF),
            pltpu.VMEM((width + 2 * head_size, length), BF),
            pltpu.VMEM((length, 2 * head_size), BF),
        ],
        compiler_params=pltpu.CompilerParams(vmem_limit_bytes=VMEM_BYTES),
        cost_estimate=pl.CostEstimate(
            flops=10 * 4 * length * length * width, bytes_accessed=6 * length * width, transcendentals=0
        ),
    )(place, qkv)


def attend_back_kernel(
    blocks,
    rows,
    heads,
    head_size,
    place,
    qkv,
    grad,
    tail_grad,
    log,
    tail_log,
    out,
    keys,
    values,
    keys_t,
    tail_kv,
    key_sum,
    value_sum,
    tail_key_sum,
    tail_value_sum,
):
    width = heads * head_size
    me = place[0]
    for j in range(blocks):
        slot = pl.ds(pl.multiple_of((me ^ j) * rows, rows), rows)
        here = pl.ds(j * rows, rows)
        block = qkv[slot, width : 2 * width]
        keys[here, :] = block
        keys_t[:width, here] = block.T
        values[here, :] = qkv[slot, 2 * width : 3 * width]
        pair = qkv[slot, 3 * width : 3 * width + 2 * head_size]
        tail_kv[here, :] = pair
        keys_t[width:, here] = pair.T
    key_row = lax.broadcasted_iota(jnp.int32, (rows, rows), 0)
    query_row = lax.broadcasted_iota(jnp.int32, (rows, rows), 1)
    scale = head_size**-0.5

    for i in range(blocks):
        slot = pl.ds(pl.multiple_of((me ^ i) * rows, rows), rows)
        query = qkv[slot, :width]
        grad_out = grad[slot, :]
        lanes = [head_lanes((rows, width), h, head_size) for h in range(heads)]
        queries = [jnp.where(m, query, jnp.zeros_like(query)) for m in lanes]
        grads = [jnp.where(m, grad_out, jnp.zeros_like(grad_out)) for m in lanes]
        query_parts = []
        for h in range(heads):
            shift = log[h : h + 1, i * rows : (i + 1) * rows]
            probs, weighted = [], []
            delta = jnp.zeros((1, rows), F32)
            for j in range(i + 1):
                here = slice(j * rows, (j + 1) * rows)
                s = dot(keys[here, :], queries[h], NT)
                if j == i:
                    s = jnp.where(key_row <= query_row, s, MASKED)
                p = jnp.exp(s - shift)
                g = dot(values[here, :], grads[h], NT)
                delta = delta + (p * g).sum(axis=0, keepdims=True)
                probs.append(p)
                weighted.append(g)
            part = jnp.zeros((head_size, rows), F32)
            for j in range(i + 1):
                here = slice(j * rows, (j + 1) * rows)
                ds = (probs[j] * (weighted[j] - delta)).astype(BF)
                p = probs[j].astype(BF)
                key_part = dot(ds, queries[h], NN)
                value_part = dot(p, grads[h], NN)
                if h == 0 and j == i:
                    key_sum[here, :] = key_part
                    value_sum[here, :] = value_part
                else:
                    key_sum[here, :] += key_part
                    value_sum[here, :] += value_part
                part = part + dot(keys_t[h * head_size : (h + 1) * head_size, here], ds, NN)
            query_parts.append(part)
        out[slot, :width] = (jnp.concatenate(query_parts, axis=0) * scale).T.astype(BF)

    query = qkv[0:rows, 3 * width + 2 * head_size : 3 * width + 3 * head_size]
    grad_out = tail_grad[...]
    probs, weighted = [], []
    delta = jnp.zeros((1, rows), F32)
    for j in range(blocks):
        here = slice(j * rows, (j + 1) * rows)
        s = dot(tail_kv[here, :head_size], query, NT)
        s = jnp.where(j * rows + key_row <= me * rows + query_row, s, MASKED)
        p = jnp.exp(s - tail_log[...])
        g = dot(tail_kv[here, head_size:], grad_out, NT)
        delta = delta + (p * g).sum(axis=0, keepdims=True)
        probs.append(p)
        weighted.append(g)
    part = jnp.zeros((head_size, rows), F32)
    for j in range(blocks):
        here = slice(j * rows, (j + 1) * rows)
        slot = pl.ds(pl.multiple_of((me ^ j) * rows, rows), rows)
        ds = (probs[j] * (weighted[j] - delta)).astype(BF)
        key_part = dot(ds, query, NN)
        value_part = dot(probs[j].astype(BF), grad_out, NN)
        part = part + dot(keys_t[width : width + head_size, here], ds, NN)
        out[slot, width : 2 * width] = key_sum[here, :].astype(BF)
        out[slot, 2 * width : 3 * width] = value_sum[here, :].astype(BF)
        out[slot, 3 * width : 3 * width + 2 * head_size] = jnp.concatenate(
            (key_part, value_part), axis=1
        ).astype(BF)
    tail_columns = slice(3 * width + 2 * head_size, 3 * width + 3 * head_size)
    out[0:rows, tail_columns] = (part * scale).T.astype(BF)
    for j in range(1, blocks):
        out[j * rows : (j + 1) * rows, tail_columns] = jnp.zeros((rows, head_size), BF)


def attend_back(place, qkv, grad, tail_grad, log, tail_log, blocks, rows, heads, head_size):
    width = heads * head_size
    length = blocks * rows
    return pl.pallas_call(
        functools.partial(attend_back_kernel, blocks, rows, heads, head_size),
        out_shape=jax.ShapeDtypeStruct(qkv.shape, BF),
        in_specs=[pl.BlockSpec(memory_space=pltpu.SMEM)]
        + [pl.BlockSpec(memory_space=pltpu.VMEM)] * 5,
        out_specs=pl.BlockSpec(memory_space=pltpu.VMEM),
        scratch_shapes=[
            pltpu.VMEM((length, width), BF),
            pltpu.VMEM((length, width), BF),
            pltpu.VMEM((width + 2 * head_size, length), BF),
            pltpu.VMEM((length, 2 * head_size), BF),
            pltpu.VMEM((length, width), F32),
            pltpu.VMEM((length, width), F32),
            pltpu.VMEM((length, head_size), F32),
            pltpu.VMEM((length, head_size), F32),
        ],
        compiler_params=pltpu.CompilerParams(vmem_limit_bytes=VMEM_BYTES),
        cost_estimate=pl.CostEstimate(
            flops=10 * 10 * length * length * width, bytes_accessed=9 * length * width, transcendentals=0
        ),
    )(place, qkv, grad, tail_grad, log, tail_log)


def mlp_kernel(
    normed, grad, up, down, bias, hidden_out, grad_pre_out, part_out, grad_part_out, bias_out
):
    pre = dot(normed[...], up[...], NN) + bias[...]
    bell = jnp.exp(-0.5 * pre * pre) * 0.3989422804014327
    below = 0.5 + 0.5 * lax.erf(pre * 0.7071067811865476)
    hidden = (pre * below).astype(BF)
    hidden_out[...] = hidden
    part_out[...] = dot(hidden, down[...], NN).astype(BF)
    grad_pre = ((below + pre * bell) * dot(grad[...], down[...], NT)).astype(BF)
    grad_pre_out[...] = grad_pre
    grad_part_out[...] = dot(grad_pre, up[...], NT).astype(BF)
    sums = grad_pre.astype(F32).sum(axis=0, keepdims=True)

    @pl.when(pl.program_id(0) == 0)
    def _():
        bias_out[...] = sums

    @pl.when(pl.program_id(0) > 0)
    def _():
        bias_out[...] += sums


def mlp(normed, grad, up, down, bias, rows):
    length, wide = normed.shape
    hidden = up.shape[1]
    row_block = pl.BlockSpec((rows, wide), lambda i: (i, 0))
    hidden_block = pl.BlockSpec((rows, hidden), lambda i: (i, 0))
    whole = pl.BlockSpec(memory_space=pltpu.VMEM)
    return pl.pallas_call(
        mlp_kernel,
        grid=(length // rows,),
        out_shape=(
            jax.ShapeDtypeStruct((length, hidden), BF),
            jax.ShapeDtypeStruct((length, hidden), BF),
            jax.ShapeDtypeStruct((length, wide), BF),
            jax.ShapeDtypeStruct((length, wide), BF),
            jax.ShapeDtypeStruct((1, hidden), F32),
        ),
        in_specs=[row_block, row_block, whole, whole, whole],
        out_specs=(
            hidden_block,
            hidden_block,
            row_block,
            row_block,
            pl.BlockSpec((1, hidden), lambda i: (0, 0)),
        ),
        compiler_params=pltpu.CompilerParams(vmem_limit_bytes=VMEM_BYTES),
        cost_estimate=pl.CostEstimate(
            flops=12 * length * wide * hidden,
            bytes_accessed=2 * (6 * length * wide + 2 * wide * hidden),
            transcendentals=0,
        ),
    )(normed, grad, up, down, bias)


def on_device(
    layer_input,
    output_grad,
    attn_gain,
    attn_shift,
    merged_weight,
    query_bias,
    value_bias,
    out_weight,
    out_bias,
    mlp_gain,
    mlp_shift,
    up_weight,
    up_bias,
    down_weight,
    down_bias,
):
    micros = layer_input.shape[0]
    rows = layer_input.shape[2]
    wide = layer_input.shape[3]
    head_size = wide // HEADS
    blocks = lax.axis_size("ctx")
    shards = lax.axis_size("fsdp")
    me = lax.axis_index("ctx")
    heads = HEADS // blocks
    width = heads * head_size
    main = blocks * width
    own = merged_weight.shape[0]
    hidden = up_weight.shape[1]
    piece = hidden // shards // blocks
    quads = hidden // wide
    used = 3 * width + 3 * head_size
    assert HEADS - heads * blocks == 1
    place = me.astype(jnp.int32).reshape(1)
    relative = jnp.arange(blocks, dtype=jnp.int32) ^ me
    start = me * width

    vectors = jnp.concatenate(
        (
            attn_gain,
            attn_shift,
            query_bias,
            value_bias,
            out_bias,
            mlp_gain,
            mlp_shift,
            down_bias,
            up_bias,
        )
    ).reshape(8 + quads, own)
    first = jnp.concatenate(
        (
            lax.dynamic_slice_in_dim(merged_weight, start, width, 1),
            lax.dynamic_slice_in_dim(merged_weight, wide + start, width, 1),
            lax.dynamic_slice_in_dim(merged_weight, 2 * wide + start, width, 1),
            merged_weight[:, wide + main : 2 * wide],
            merged_weight[:, 2 * wide + main :],
            merged_weight[:, main:wide],
            vectors.T,
        ),
        axis=1,
    )
    first = lax.all_gather(first, "fsdp", axis=0, tiled=True)
    merged_own = first[:, :used]
    vectors = first[:, used:].T.astype(F32)
    gain_one, shift_one, query_row, value_row, out_row, gain_two, shift_two, down_row = [
        vectors[i] for i in range(8)
    ]
    up_row = (
        vectors[8:]
        .reshape(quads, shards, own)
        .transpose(1, 0, 2)
        .reshape(shards, blocks, piece)
    )
    up_row = lax.dynamic_index_in_dim(up_row, me, 1, keepdims=False).reshape(1, shards * piece)
    zero_tail = jnp.zeros((head_size,), F32)
    merged_row = jnp.concatenate(
        (
            lax.dynamic_slice_in_dim(query_row, start, width),
            jnp.zeros((width,), F32),
            lax.dynamic_slice_in_dim(value_row, start, width),
            zero_tail,
            value_row[main:],
            query_row[main:],
        )
    )
    scale_row = jnp.concatenate(
        (
            jnp.full((width,), head_size**-0.5, BF),
            jnp.ones((2 * width + 2 * head_size,), BF),
            jnp.full((head_size,), head_size**-0.5, BF),
        )
    )
    out_full = lax.all_gather(out_weight, "fsdp", axis=0, tiled=True)
    up_own = lax.dynamic_index_in_dim(
        up_weight.reshape(own, shards, blocks, piece), me, 2, keepdims=False
    ).reshape(own, shards * piece)
    down_own = lax.dynamic_slice_in_dim(down_weight, me * piece, piece, 0)
    up_own = lax.all_gather(up_own, "fsdp", axis=0, tiled=True)
    down_own = lax.all_gather(down_own, "fsdp", axis=0, tiled=True)

    values = [layer_input[m, 0] for m in range(micros)]
    values_ctx = [gather_ctx(v) for v in values]
    grads = [output_grad[m, 0] for m in range(micros)]
    grads_ctx = [jnp.concatenate(gather_ctx(g)) for g in grads]

    unscaled, normed, qkv, log, tail_log, attended, middle, normed_two = ([] for _ in range(8))
    for m in range(micros):
        centred, rate = normal(jnp.concatenate(values_ctx[m]).astype(F32))
        unscaled.append((centred, rate))
        normed.append((centred * gain_one + shift_one).astype(BF))
        rows_out = jnp.dot(normed[m], merged_own, preferred_element_type=F32) + merged_row
        qkv.append(rows_out.astype(BF) * scale_row)
        out, tail_out, total, tail_total = attend(place, qkv[m], blocks, rows, heads, head_size)
        log.append(total)
        tail_log.append(tail_total)
        traded = jnp.stack(trade_ctx(list(out.reshape(blocks, rows, width))))
        traded = jnp.take(traded, relative, axis=0).transpose(1, 0, 2).reshape(rows, main)
        attended.append(jnp.concatenate((traded, tail_out), axis=1))
        middle.append(
            values[m].astype(F32)
            + jnp.dot(attended[m], out_full, preferred_element_type=F32)
            + out_row
        )
        centred, rate = normal(middle[m])
        normed_two.append((centred * gain_two + shift_two).astype(BF))

    hiddens, grad_pres, normed_two_ctx, layer_output, grad_middle = ([] for _ in range(5))
    grad_up_row = 0.0
    grad_gain_two = 0.0
    grad_shift_two = 0.0
    for m in range(micros):
        normed_two_ctx.append(jnp.concatenate(gather_ctx(normed_two[m])))
        act, grad_pre, part, grad_part, bias_part = mlp(
            normed_two_ctx[m], grads_ctx[m], up_own, down_own, up_row, rows
        )
        hiddens.append(act)
        grad_pres.append(grad_pre)
        grad_up_row = grad_up_row + bias_part
        grad_normed = reduce_ctx(list(grad_part.reshape(blocks, rows, wide)))
        centred, rate = normal(middle[m])
        grad_gain_two = grad_gain_two + jnp.sum(grad_normed * centred, axis=0)
        grad_shift_two = grad_shift_two + jnp.sum(grad_normed, axis=0)
        grad_middle.append(
            grads[m].astype(F32) + norm_back(centred, rate, grad_normed * gain_two)
        )
        total = reduce_ctx(list(part.reshape(blocks, rows, wide)))
        layer_output.append((middle[m] + total + down_row).astype(BF))
    grad_down = sum(dot(a, g, ((0,), (0,))) for a, g in zip(hiddens, grads_ctx, strict=True))
    grad_up = sum(dot(n, g, ((0,), (0,))) for n, g in zip(normed_two_ctx, grad_pres, strict=True))
    grad_down = lax.psum_scatter(grad_down.astype(BF), "fsdp", scatter_dimension=0, tiled=True)
    grad_up = lax.psum_scatter(grad_up.astype(BF), "fsdp", scatter_dimension=0, tiled=True)

    grad_out_weight = 0.0
    grad_out_row = 0.0
    grad_down_row = 0.0
    grad_merged = 0.0
    grad_merged_row = 0.0
    grad_gain_one = 0.0
    grad_shift_one = 0.0
    input_grad = []
    for m in range(micros):
        grad_attn = grad_middle[m].astype(BF)
        grad_out_weight = grad_out_weight + dot(attended[m], grad_attn, ((0,), (0,)))
        grad_out_row = grad_out_row + jnp.sum(grad_attn.astype(F32), axis=0)
        grad_down_row = grad_down_row + jnp.sum(grads[m].astype(F32), axis=0)
        grad_attended = dot(grad_attn, out_full, NT).astype(BF)
        to_trade = grad_attended[:, :main].reshape(rows, blocks, width).transpose(1, 0, 2)
        to_trade = jnp.take(to_trade, relative, axis=0)
        traded = jnp.concatenate(trade_ctx(list(to_trade)))
        grad_qkv = attend_back(
            place,
            qkv[m],
            traded,
            grad_attended[:, main:],
            log[m],
            tail_log[m],
            blocks,
            rows,
            heads,
            head_size,
        )
        grad_merged = grad_merged + dot(normed[m], grad_qkv, ((0,), (0,)))
        grad_merged_row = grad_merged_row + jnp.sum(grad_qkv.astype(F32), axis=0)
        grad_part = dot(grad_qkv, merged_own, NT)
        centred, rate = unscaled[m]
        grad_gain_one = grad_gain_one + jnp.sum(grad_part * centred, axis=0)
        grad_shift_one = grad_shift_one + jnp.sum(grad_part, axis=0)
        grad_normed = reduce_ctx(list(grad_part.astype(BF).reshape(blocks, rows, wide)))
        input_grad.append(
            grad_middle[m] + norm_back(centred[:rows], rate[:rows], grad_normed * gain_one)
        )

    def placed(part, tail):
        row = lax.dynamic_update_slice_in_dim(jnp.zeros((main,), F32), part, start, 0)
        return jnp.concatenate((row, tail))

    up_sums = lax.dynamic_update_slice_in_dim(
        jnp.zeros((shards, blocks, piece), F32), grad_up_row.reshape(shards, 1, piece), me, 1
    )
    up_sums = up_sums.reshape(shards, quads, own).transpose(1, 0, 2).reshape(quads, wide)
    vector_sums = jnp.concatenate(
        (
            jnp.stack(
                (
                    grad_gain_one,
                    grad_shift_one,
                    placed(grad_merged_row[:width], grad_merged_row[used - head_size :]),
                    placed(
                        grad_merged_row[2 * width : 3 * width],
                        grad_merged_row[3 * width + head_size : 3 * width + 2 * head_size],
                    ),
                    grad_out_row,
                    grad_gain_two,
                    grad_shift_two,
                    grad_down_row,
                )
            ),
            up_sums,
        )
    )
    last = jnp.concatenate((grad_merged, vector_sums.T), axis=1).astype(BF)
    last = lax.psum_scatter(last, "fsdp", scatter_dimension=0, tiled=True)
    grad_out_weight = lax.psum_scatter(
        grad_out_weight.astype(BF), "fsdp", scatter_dimension=0, tiled=True
    ).astype(F32)
    bit = 1
    while bit < blocks:
        grad_out_weight = grad_out_weight + swap(grad_out_weight.astype(BF), bit).astype(F32)
        bit *= 2

    def absolute(parts):
        return jnp.take(jnp.stack(parts), relative, axis=0).astype(F32)

    last = absolute(gather_ctx(last))
    tails = jnp.sum(last[:, :, 3 * width :], axis=0)

    def columns(index, tail):
        body = last[:, :, index * width : (index + 1) * width].transpose(1, 0, 2)
        return [body.reshape(own, main), tails[:, tail * head_size : (tail + 1) * head_size]]

    grad_merged = jnp.concatenate(columns(0, 2) + columns(1, 0) + columns(2, 1), axis=1)
    vector_sums = tails[:, 3 * head_size :].T
    grad_up = absolute(gather_ctx(grad_up)).reshape(blocks, own, shards, piece)
    grad_up = grad_up.transpose(1, 2, 0, 3).reshape(own, hidden)
    grad_down = absolute(gather_ctx(grad_down)).reshape(blocks * piece, wide)
    return (
        jnp.stack(layer_output)[:, None],
        jnp.stack(input_grad)[:, None],
        vector_sums[0],
        vector_sums[1],
        grad_merged,
        vector_sums[2],
        vector_sums[3],
        grad_out_weight,
        vector_sums[4],
        vector_sums[5],
        vector_sums[6],
        grad_up,
        vector_sums[8:].reshape(quads * own),
        grad_down,
        vector_sums[7],
    )


def solution(mesh):
    rows = P(None, "fsdp", "ctx", None)
    matrix = P("fsdp", None)
    vector = P("fsdp")
    in_specs = (
        rows,
        rows,
        vector,
        vector,
        matrix,
        vector,
        vector,
        matrix,
        vector,
        vector,
        vector,
        matrix,
        vector,
        matrix,
        vector,
    )
    out_specs = (rows, rows) + in_specs[2:]
    return jax.shard_map(
        on_device, mesh=mesh, in_specs=in_specs, out_specs=out_specs, check_vma=False
    )
```

time: 1210 us -> 582 us (0.48)
  waiting for transfers between devices: 728 us -> 43.8 us
  local copies, waits for them, and re-layouts: 51.9 us -> 189 us
  matrix products: 186 us -> 67.9 us
  blocking collectives: 102 us -> 0 us
  Pallas kernels: 0 us -> 97.6 us
  starting transfers between devices: 49.9 us -> 86.8 us
  other arithmetic: 57.6 us -> 76.9 us
    reduce_scatter x6 -> x0, waiting for transfers between devices: 234 us -> none  [the longest x2 158 us: on_device(): lax.psum_scatter(grad_merged.astype(jnp.bfloat16), 'fsdp', scatter_dimens...]
    ppermute x14 -> x74, waiting for transfers between devices: 260 us -> 42.9 us  [swap(): return lax.ppermute(block, 'ctx', [(i, i ^ bit) for i in range(size)])]
    unnamed x24 -> x12, waiting for transfers between devices: 132 us -> 0.84 us
    dot_general x38 -> x16, matrix products: 186 us -> 67.9 us  [the longest x12 52.6 us: dot(): lax.dot_general(a, b, ((dims[0], dims[1]), ((), ())), preferred_element_t...]
    all_gather x6 -> x4, waiting for transfers between devices: 103 us -> 0.03 us  [the longest x1 0.02 us: on_device(): out_full = lax.all_gather(out_weight, 'fsdp', axis=0, tiled=True)]
    pallas_call x0 -> x6, Pallas kernels: none -> 97.6 us  [the longest x2 38.5 us: mlp(): pl.pallas_call(mlp_kernel, grid=(length // rows,), out_shape=(jax.ShapeDt...]
    unnamed x2 -> x0, blocking collectives: 59 us -> none
    ppermute x0 -> x24, local copies, waits for them, and re-layouts: none -> 38.7 us  [swap(): return lax.ppermute(block, 'ctx', [(i, i ^ bit) for i in range(size)])]
  transfers between devices with their start and end apart: 32 -> 82, of which waited for: 27 -> 18; matrix products, arithmetic and copies ran while one was open for 23% -> 53% of each run, Pallas kernels for 0% -> 14%
where the time goes in v1:
time: 582 us; the launch traced here: 579 us
  local copies, waits for them, and re-layouts  189 us (32%)
  Pallas kernels  97.6 us (17%)
  starting transfers between devices  86.8 us (15%)
  other arithmetic  76.9 us (13%)
  matrix products  67.9 us (12%)
  waiting for transfers between devices  43.8 us (8%)
  between operations  16.5 us (3%)
    ppermute x74, starting transfers between devices, swap(): return lax.ppermute(block, 'ctx', [(i, i ^ bit) for i in range(size)])  86 us
    dot_general x12, matrix products, dot(): lax.dot_general(a, b, ((dims[0], dims[1]), ((), ())), preferred_element_t...  52.6 us
    ppermute x74, waiting for transfers between devices, swap(): return lax.ppermute(block, 'ctx', [(i, i ^ bit) for i in range(size)])  42.9 us
    ppermute x24, local copies, waits for them, and re-layouts, swap(): return lax.ppermute(block, 'ctx', [(i, i ^ bit) for i in range(size)])  38.7 us
    pallas_call x2, Pallas kernels, mlp(): pl.pallas_call(mlp_kernel, grid=(length // rows,), out_shape=(jax.ShapeDt...  38.5 us
    unnamed x208, local copies, waits for them, and re-layouts  35.3 us
    pallas_call x2, Pallas kernels, attend(): pl.pallas_call(functools.partial(attend_kernel, blocks, rows, heads, head...  30.8 us
    pallas_call x2, Pallas kernels, attend_back(): pl.pallas_call(functools.partial(attend_back_kernel, blocks, rows, heads,...  28.3 us
  transfers between devices with their start and end apart: 82, of which 18 were waited for; matrix products, arithmetic and copies ran while one was open for 53% of the time, Pallas kernels for 14%

profile of v1, /device:TPU:0, one launch (start us, length us, event | category | flops | bytes accessed | tf_op | source)
XLA Modules:
  0.0 578.5 jit_solution(14550188171034671196)
XLA Ops:
  8.3 6.1 %concatenate.104 = bf16[1632]{0:T(1024)(128)(2,1)S(1)} concatenate(bf16[136]{0:T(256)(128)(2,1)} %param.21, bf16[136]{0:T(256)(128)(2,1)} %param.22, bf16[136]{0:T(256)(128)(2,1)} %param.24, bf16[136]{0:T(256)(128)(2,1)} %param.25, bf16[136]{0:T(256)(128)(2,1)} %param.27, bf16[136]{0:T(256)(128)(2,1)} %param.28, bf16[136]{0:T(256)(128)(2,1)} %param.29, bf16[136]{0:T(256)(128)(2,1)} %param.33, ...), dimensions={0} | concatenate | bytes 6528 | tf_op jit(solution)/shard_map/concatenate | solution.py:404
  19.6 2.9 collective-permute-start.19
  28.0 7.8 %reshape.414 = bf16[136,8,4,136]{3,2,1,0:T(4,128)(2,1)S(1)} reshape(bf16[136,4352]{1,0:T(8,128)(2,1)} %param.30) | data formatting | bytes 2367488 | tf_op jit(solution)/shard_map/reshape | solution.py:462
  35.8 3.4 dynamic-slice_reduce_fusion
  65.8 6.3 %collective-permute-done.11 = bf16[256,1088]{0,1:T(8,128)(2,1)} collective-permute-done((bf16[256,1088]{0,1:T(8,128)(2,1)}, bf16[256,1088]{0,1:T(8,128)(2,1)}, u32[]{:S(2)}, u32[]{:S(2)}) %collective-permute-start.11) | collective-permute-done | bytes 557088 | tf_op jit(solution)/shard_map/ppermute | solution.py:20
  75.2 2.1 copy.106
  89.3 2.4 collective-permute-done.2
  96.8 6.6 %fusion.12.qkv = bf16[1024,960]{1,0:T(8,128)(2,1)} fusion(f32[960]{0:T(1024)S(1)} %concatenate.106, bf16[1088,972]{1,0:T(8,128)(2,1)} %all-gather.5.cloned.1.call-done, bf16[960]{0:T(1024)(128)(2,1)S(1)} %copy-done.87, f32[1088]{0:T(1024)S(1)} %get-tuple-element.196, f32[1088]{0:T(1024)S(1)} %get-tuple-element.195, bf16[1024,1088]{1,0:T(8,128)(2,1)} %copy-done.8, ...), kind=kOutput, calls=%fused_computation.41 | convolution fusion | flops 2148728832 | bytes 6332032 | tf_op jit(solution)/shard_map/dot_general | solution.py:478
  103.5 21.9 %shard_map.264 = (bf16[1024,256]{1,0:T(8,128)(2,1)}, bf16[256,64]{1,0:T(8,128)(2,1)}, f32[4,1024]{1,0:T(4,128)}, f32[1,256]{1,0:T(1,128)}) custom-call(s32[1]{0:T(128)} %bitcast.1.place, bf16[1024,960]{1,0:T(8,128)(2,1)} %fusion.12.qkv), custom_call_target="tpu_custom_call" | custom-call | flops 10737418240 | bytes 1572864 | tf_op jit(solution)/shard_map/pallas_call | solution.py:152
  130.3 4.5 fusion.11.qkv
  134.8 8.9 %shard_map.262 = (bf16[1024,256]{1,0:T(8,128)(2,1)}, bf16[256,64]{1,0:T(8,128)(2,1)}, f32[4,1024]{1,0:T(4,128)}, f32[1,256]{1,0:T(1,128)}) custom-call(s32[1]{0:T(128)} %bitcast.1.place, bf16[1024,960]{1,0:T(8,128)(2,1)} %fusion.11.qkv), custom_call_target="tpu_custom_call" | custom-call | flops 10737418240 | bytes 1572864 | tf_op jit(solution)/shard_map/pallas_call | solution.py:152
  156.7 3.0 fusion.55
  175.0 5.0 collective-permute-done.26
  187.3 2.4 collective-permute-done.7
  200.7 19.1 %shard_map.265 = (bf16[1024,1088]{1,0:T(8,128)(2,1)}, bf16[1024,1088]{1,0:T(8,128)(2,1)}, bf16[1024,1088]{1,0:T(8,128)(2,1)}, bf16[1024,1088]{1,0:T(8,128)(2,1)}, f32[1,1088]{1,0:T(1,128)}) custom-call(bf16[1024,1088]{1,0:T(8,128)(2,1)} %constant_dynamic-update-slice_fusion.17.normed, bf16[1024,1088]{1,0:T(8,128)(2,1)} %constant_dynamic-update-slice_fusion.22.grad, ...), custom_call_target="tpu_custom_call" | custom-call | flops 14545846272 | bytes 18104320 | tf_op jit(solution)/shard_map/pallas_call | solution.py:340
  219.9 7.0 %fusion.58 = f32[1088,1088]{1,0:T(8,128)} fusion(bf16[1024,1088]{1,0:T(8,128)(2,1)S(1)} %copy-done.55, bf16[1024,1088]{1,0:T(8,128)(2,1)} %get-tuple-element.50), kind=kOutput, calls=%fused_computation.257 | convolution fusion | flops 2424307712 | bytes 9191424 | tf_op jit(solution)/shard_map/dot_general | solution.py:80
  228.4 19.3 %shard_map.263 = (bf16[1024,1088]{1,0:T(8,128)(2,1)}, bf16[1024,1088]{1,0:T(8,128)(2,1)}, bf16[1024,1088]{1,0:T(8,128)(2,1)}, bf16[1024,1088]{1,0:T(8,128)(2,1)}, f32[1,1088]{1,0:T(1,128)}) custom-call(bf16[1024,1088]{1,0:T(8,128)(2,1)} %constant_dynamic-update-slice_fusion.4.normed, bf16[1024,1088]{1,0:T(8,128)(2,1)} %constant_dynamic-update-slice_fusion.9.grad, ...), custom_call_target="tpu_custom_call" | custom-call | flops 14545846272 | bytes 18104320 | tf_op jit(solution)/shard_map/pallas_call | solution.py:340
  247.7 7.7 %fusion.1 = bf16[1088,1088]{1,0:T(8,128)(2,1)} fusion(f32[1088,1088]{1,0:T(8,128)} %fusion.58, bf16[1024,1088]{1,0:T(8,128)(2,1)S(1)} %copy-done.54, bf16[1024,1088]{1,0:T(8,128)(2,1)} %get-tuple-element.49), kind=kOutput, calls=%fused_computation.11 | convolution fusion | flops 2426675200 | bytes 11558912 | tf_op jit(solution)/shard_map/dot_general | solution.py:80
  255.6 2.3 fusion.47
  266.5 5.7 fusion.59
  272.3 4.7 fusion.2
  277.3 2.3 fusion.48
  281.3 2.1 add_convert_fusion.16
  285.4 3.6 collective-permute-done.40
  289.4 2.2 add_convert_fusion.20
  298.2 2.2 add_convert_fusion.22
  312.6 2.1 copy.153
  315.4 2.1 copy.155
  323.1 2.1 copy.144
  325.3 3.2 multiply_reduce_fusion.3
  328.5 2.1 copy.138
  330.6 4.9 collective-permute-done.37
  335.5 2.1 copy.140
  337.6 4.1 convert_reduce_fusion.6
  343.4 2.1 copy.110
  345.5 2.1 copy.112
  347.6 4.0 convert_reduce_fusion.7
  364.6 14.0 %shard_map.267 = bf16[1024,960]{1,0:T(8,128)(2,1)} custom-call(s32[1]{0:T(128)} %bitcast.1.place, bf16[1024,960]{1,0:T(8,128)(2,1)} %fusion.12.qkv, bf16[1024,256]{1,0:T(8,128)(2,1)} %pad_maximum_fusion.21.grad, bf16[256,64]{1,0:T(8,128)(2,1)} %slice.561.tail_grad, f32[4,1024]{1,0:T(4,128)} %get-tuple-element.45.log, f32[1,256]{1,0:T(1,128)} %get-tuple-element.46.tail_log), custom_call_target="tpu_custom_call" | custom-call | flops 26843545600 | bytes 2359296 | tf_op jit(solution)/shard_map/pallas_call | solution.py:288
  381.5 14.3 %shard_map.266 = bf16[1024,960]{1,0:T(8,128)(2,1)} custom-call(s32[1]{0:T(128)} %bitcast.1.place, bf16[1024,960]{1,0:T(8,128)(2,1)} %fusion.11.qkv, bf16[1024,256]{1,0:T(8,128)(2,1)} %pad_maximum_fusion.20.grad, bf16[256,64]{1,0:T(8,128)(2,1)} %slice.552.tail_grad, f32[4,1024]{1,0:T(4,128)} %get-tuple-element.42.log, f32[1,256]{1,0:T(1,128)} %get-tuple-element.43.tail_log), custom_call_target="tpu_custom_call" | custom-call | flops 26843545600 | bytes 2359296 | tf_op jit(solution)/shard_map/pallas_call | solution.py:288
  398.2 4.6 fusion.57
  402.8 4.7 fusion.56
  407.5 6.3 %copy.158 = f32[1024,1088]{1,0:T(8,128)} copy(f32[1024,1088]{0,1:T(8,128)} %get-tuple-element.251) | data formatting | bytes 8912896 | tf_op jit(solution)/shard_map/dot_general | solution.py:80
  413.8 5.9 %copy.147 = f32[1024,1088]{1,0:T(8,128)} copy(f32[1024,1088]{0,1:T(8,128)} %get-tuple-element.249) | data formatting | bytes 8912896 | tf_op jit(solution)/shard_map/dot_general | solution.py:80
  419.7 7.7 %multiply_reduce_fusion = (f32[1088]{0:T(1024)S(1)}, bf16[1024,1088]{1,0:T(8,128)(2,1)}, f32[1024,1088]{1,0:T(8,128)}) fusion(f32[1024,1088]{1,0:T(8,128)} %copy.158, f32[1024]{0:T(1024)S(1)} %copy-done.70, f32[1024]{0:T(1024)S(1)} %copy-done.64, bf16[1024,1088]{1,0:T(8,128)(2,1)} %copy-done.8), kind=kLoop, calls=%fused_computation.23 | loop fusion | flops 6683584 | bytes 13381888 | tf_op jit(solution)/shard_map/reduce_sum | solution.py:553
  428.7 3.4 multiply_reduce_fusion.1
  432.3 4.9 fusion.19
  437.2 3.1 add_convert_fusion.2
  440.5 2.5 copy.180
  444.0 3.1 fusion.23
  451.5 5.7 collective-permute-done.56
  471.7 4.9 fusion
  478.0 2.1 copy.162
  480.1 2.1 copy.149
  482.2 2.1 copy.151
  484.3 3.7 fusion.24
  490.3 4.8 add_bitcast_fusion.1
  500.3 3.2 maximum_bitcast_fusion
  503.5 3.1 copy.173
  520.7 2.4 collective-permute-start.60
  523.1 3.1 broadcast_select_fusion
  527.8 2.3 collective-permute-start.62
  534.1 5.8 reshape.438
  539.8 7.2 %copy.171 = f32[136,8,4,136]{3,2,1,0:T(4,128)} copy(f32[136,8,4,136]{3,1,0,2:T(8,128)} %bitcast.149) | data formatting | bytes 4734976 | tf_op jit(solution)/shard_map/reshape | solution.py:611
  547.0 6.2 %reshape.433 = f32[136,4352]{1,0:T(8,128)} reshape(f32[136,8,4,136]{3,2,1,0:T(4,128)} %copy.171) | data formatting | bytes 4734976 | tf_op jit(solution)/shard_map/reshape | solution.py:611
  (578 shorter events, 236.3 us)
Async XLA Ops:
  7.2 86.0 %all-gather.5.cloned.1.call-start = ((), (), s32[]{:S(2)}) async-start(), calls=%async_computation.4 | async-start | bytes 2506752 | tf_op jit(solution)/shard_map/all_gather | solution.py:429
  16.7 139.6 %all-gather.7.cloned.1.call-start = ((), (), s32[]{:S(2)}) async-start(), calls=%async_computation.5 | async-start | bytes 2820096 | tf_op jit(solution)/shard_map/all_gather | solution.py:460
  17.4 183.3 %all-gather.11.cloned.1.call-start = ((), (), s32[]{:S(2)}) async-start(), calls=%async_computation.7 | async-start | bytes 2820096 | tf_op jit(solution)/shard_map/all_gather | solution.py:466
  18.3 182.4 %all-gather.9.cloned.1.call-start = ((), (), s32[]{:S(2)}) async-start(), calls=%async_computation.6 | async-start | bytes 2820096 | tf_op jit(solution)/shard_map/all_gather | solution.py:465
  19.6 27.6 %collective-permute-start.19 = (bf16[256,1088]{0,1:T(8,128)(2,1)}, bf16[256,1088]{0,1:T(8,128)(2,1)}, u32[]{:S(2)}, u32[]{:S(2)}) collective-permute-start(bf16[256,1088]{0,1:T(8,128)(2,1)} %get-tuple-element.182), channel_id=1, source_target_pairs={{0,8},{8,0},{16,24},{24,16},{1,9},{9,1},{17,25},{25,17},{2,10},{10... | collective-permute-start | bytes 1671176 | tf_op jit(solution)/shard_map/ppermute | solution.py:20
  22.5 28.4 %collective-permute-start.20 = (bf16[256,1088]{0,1:T(8,128)(2,1)}, bf16[256,1088]{0,1:T(8,128)(2,1)}, u32[]{:S(2)}, u32[]{:S(2)}) collective-permute-start(bf16[256,1088]{0,1:T(8,128)(2,1)} %get-tuple-element.182), channel_id=1, source_target_pairs={{0,16},{8,24},{16,0},{24,8},{1,17},{9,25},{17,1},{25,9},{2,18},{10... | collective-permute-start | bytes 1671176 | tf_op jit(solution)/shard_map/ppermute | solution.py:20
  24.1 28.8 %collective-permute-start = (bf16[256,1088]{0,1:T(8,128)(2,1)}, bf16[256,1088]{0,1:T(8,128)(2,1)}, u32[]{:S(2)}, u32[]{:S(2)}) collective-permute-start(bf16[256,1088]{0,1:T(8,128)(2,1)} %get-tuple-element.181), channel_id=1, source_target_pairs={{0,8},{8,0},{16,24},{24,16},{1,9},{9,1},{17,25},{25,17},{2,10},{10... | collective-permute-start | bytes 1671176 | tf_op jit(solution)/shard_map/ppermute | solution.py:20
  24.6 32.9 %collective-permute-start.1 = (bf16[256,1088]{0,1:T(8,128)(2,1)}, bf16[256,1088]{0,1:T(8,128)(2,1)}, u32[]{:S(2)}, u32[]{:S(2)}) collective-permute-start(bf16[256,1088]{0,1:T(8,128)(2,1)} %get-tuple-element.181), channel_id=1, source_target_pairs={{0,16},{8,24},{16,0},{24,8},{1,17},{9,25},{17,1},{25,9},{2,18},{10... | collective-permute-start | bytes 1671176 | tf_op jit(solution)/shard_map/ppermute | solution.py:20
  26.0 34.8 %collective-permute-start.30 = (bf16[256,1088]{0,1:T(8,128)(2,1)}, bf16[256,1088]{0,1:T(8,128)(2,1)}, u32[]{:S(2)}, u32[]{:S(2)}) collective-permute-start(bf16[256,1088]{0,1:T(8,128)(2,1)} %get-tuple-element.178), channel_id=1, source_target_pairs={{0,8},{8,0},{16,24},{24,16},{1,9},{9,1},{17,25},{25,17},{2,10},{10... | collective-permute-start | bytes 1671176 | tf_op jit(solution)/shard_map/ppermute | solution.py:20
  40.5 447.5 %reduce-scatter.17.cloned.1.call-start = ((), (), s32[]{:S(2)}) async-start(), calls=%async_computation.10 | async-start | bytes 2820096
  47.2 18.4 %collective-permute-start.31 = (bf16[256,1088]{0,1:T(8,128)(2,1)}, bf16[256,1088]{0,1:T(8,128)(2,1)S(1)}, u32[]{:S(2)}, u32[]{:S(2)}) collective-permute-start(bf16[256,1088]{0,1:T(8,128)(2,1)} %get-tuple-element.178), channel_id=1, source_target_pairs={{0,16},{8,24},{16,0},{24,8},{1,17},{9,25},{17,1},{25,9},{2,18},{10... | collective-permute-start | bytes 1671176 | tf_op jit(solution)/shard_map/ppermute | solution.py:20
  51.0 21.1 %collective-permute-start.11 = (bf16[256,1088]{0,1:T(8,128)(2,1)}, bf16[256,1088]{0,1:T(8,128)(2,1)}, u32[]{:S(2)}, u32[]{:S(2)}) collective-permute-start(bf16[256,1088]{0,1:T(8,128)(2,1)} %get-tuple-element.177), channel_id=1, source_target_pairs={{0,8},{8,0},{16,24},{24,16},{1,9},{9,1},{17,25},{25,17},{2,10},{10... | collective-permute-start | bytes 1671176 | tf_op jit(solution)/shard_map/ppermute | solution.py:20
  52.9 22.3 %collective-permute-start.12 = (bf16[256,1088]{0,1:T(8,128)(2,1)}, bf16[256,1088]{0,1:T(8,128)(2,1)}, u32[]{:S(2)}, u32[]{:S(2)}) collective-permute-start(bf16[256,1088]{0,1:T(8,128)(2,1)} %get-tuple-element.177), channel_id=1, source_target_pairs={{0,16},{8,24},{16,0},{24,8},{1,17},{9,25},{17,1},{25,9},{2,18},{10... | collective-permute-start | bytes 1671176 | tf_op jit(solution)/shard_map/ppermute | solution.py:20
  57.5 28.3 %collective-permute-start.21 = (bf16[128,1088]{1,0:T(8,128)(2,1)}, bf16[128,1088]{1,0:T(8,128)(2,1)}, u32[]{:S(2)}, u32[]{:S(2)}) collective-permute-start(bf16[128,1088]{1,0:T(8,128)(2,1)} %slice.545), channel_id=1, source_target_pairs={{0,8},{8,0},{16,24},{24,16},{1,9},{9,1},{17,25},{25,17},{2,10},{10... | collective-permute-start | bytes 835592 | tf_op jit(solution)/shard_map/ppermute | solution.py:20
  60.9 26.0 %collective-permute-start.22 = (bf16[128,1088]{1,0:T(8,128)(2,1)}, bf16[128,1088]{1,0:T(8,128)(2,1)}, u32[]{:S(2)}, u32[]{:S(2)}) collective-permute-start(bf16[128,1088]{1,0:T(8,128)(2,1)} %slice.546), channel_id=1, source_target_pairs={{0,16},{8,24},{16,0},{24,8},{1,17},{9,25},{17,1},{25,9},{2,18},{10... | collective-permute-start | bytes 835592 | tf_op jit(solution)/shard_map/ppermute | solution.py:20
  81.7 10.0 %collective-permute-start.2 = (bf16[128,1088]{1,0:T(8,128)(2,1)S(1)}, bf16[128,1088]{1,0:T(8,128)(2,1)S(1)}, u32[]{:S(2)}, u32[]{:S(2)}) collective-permute-start(bf16[128,1088]{1,0:T(8,128)(2,1)S(1)} %slice.526), channel_id=1, source_target_pairs={{0,8},{8,0},{16,24},{24,16},{1,9},{9,1},{17,25},{25,17},{2,10},{10... | collective-permute-start | bytes 835592 | tf_op jit(solution)/shard_map/ppermute | solution.py:20
  85.3 61.5 %collective-permute-start.32 = (bf16[128,1088]{1,0:T(8,128)(2,1)S(1)}, bf16[128,1088]{1,0:T(8,128)(2,1)S(1)}, u32[]{:S(2)}, u32[]{:S(2)}) collective-permute-start(bf16[128,1088]{1,0:T(8,128)(2,1)S(1)} %slice.549), channel_id=1, source_target_pairs={{0,8},{8,0},{16,24},{24,16},{1,9},{9,1},{17,25},{25,17},{2,10},{10... | collective-permute-start | bytes 835592 | tf_op jit(solution)/shard_map/ppermute | solution.py:20
  126.6 21.6 %collective-permute-start.23 = (bf16[256,256]{1,0:T(8,128)(2,1)S(1)}, bf16[256,256]{1,0:T(8,128)(2,1)S(1)}, u32[]{:S(2)}, u32[]{:S(2)}) collective-permute-start(bf16[256,256]{1,0:T(8,128)(2,1)S(1)} %get-tuple-element.216), channel_id=1, source_target_pairs={{0,8},{8,0},{16,24},{24,16},{1,9},{9,1},{17,25},{25,17},{2,10},{10... | collective-permute-start | bytes 393224 | tf_op jit(solution)/shard_map/ppermute | solution.py:20
  128.7 21.5 %collective-permute-start.24 = (bf16[256,256]{1,0:T(8,128)(2,1)S(1)}, bf16[256,256]{1,0:T(8,128)(2,1)S(1)}, u32[]{:S(2)}, u32[]{:S(2)}) collective-permute-start(bf16[256,256]{1,0:T(8,128)(2,1)S(1)} %get-tuple-element.215), channel_id=1, source_target_pairs={{0,16},{8,24},{16,0},{24,8},{1,17},{9,25},{17,1},{25,9},{2,18},{10... | collective-permute-start | bytes 393224 | tf_op jit(solution)/shard_map/ppermute | solution.py:20
  130.2 22.0 %collective-permute-start.25 = (bf16[256,256]{1,0:T(8,128)(2,1)S(1)}, bf16[256,256]{1,0:T(8,128)(2,1)S(1)}, u32[]{:S(2)}, u32[]{:S(2)}) collective-permute-start(bf16[256,256]{1,0:T(8,128)(2,1)S(1)} %get-tuple-element.214), channel_id=1, source_target_pairs={{0,24},{8,16},{16,8},{24,0},{1,25},{9,17},{17,9},{25,1},{2,26},{10... | collective-permute-start | bytes 393224 | tf_op jit(solution)/shard_map/ppermute | solution.py:20
  150.2 14.7 %collective-permute-start.33 = (bf16[128,1088]{1,0:T(8,128)(2,1)}, bf16[128,1088]{1,0:T(8,128)(2,1)}, u32[]{:S(2)}, u32[]{:S(2)}) collective-permute-start(bf16[128,1088]{1,0:T(8,128)(2,1)} %slice.550), channel_id=1, source_target_pairs={{0,16},{8,24},{16,0},{24,8},{1,17},{9,25},{17,1},{25,9},{2,18},{10... | collective-permute-start | bytes 835592 | tf_op jit(solution)/shard_map/ppermute | solution.py:20
  152.2 17.4 %collective-permute-start.13 = (bf16[128,1088]{1,0:T(8,128)(2,1)}, bf16[128,1088]{1,0:T(8,128)(2,1)}, u32[]{:S(2)}, u32[]{:S(2)}) collective-permute-start(bf16[128,1088]{1,0:T(8,128)(2,1)} %slice.541), channel_id=1, source_target_pairs={{0,8},{8,0},{16,24},{24,16},{1,9},{9,1},{17,25},{25,17},{2,10},{10... | collective-permute-start | bytes 835592 | tf_op jit(solution)/shard_map/ppermute | solution.py:20
  154.3 17.0 %collective-permute-start.14 = (bf16[128,1088]{1,0:T(8,128)(2,1)}, bf16[128,1088]{1,0:T(8,128)(2,1)}, u32[]{:S(2)}, u32[]{:S(2)}) collective-permute-start(bf16[128,1088]{1,0:T(8,128)(2,1)} %slice.542), channel_id=1, source_target_pairs={{0,16},{8,24},{16,0},{24,8},{1,17},{9,25},{17,1},{25,9},{2,18},{10... | collective-permute-start | bytes 835592 | tf_op jit(solution)/shard_map/ppermute | solution.py:20
  164.1 15.9 %collective-permute-start.26 = (bf16[256,1088]{0,1:T(8,128)(2,1)}, bf16[256,1088]{0,1:T(8,128)(2,1)}, u32[]{:S(2)}, u32[]{:S(2)}) collective-permute-start(bf16[256,1088]{0,1:T(8,128)(2,1)} %copy.124), channel_id=1, source_target_pairs={{0,8},{8,0},{16,24},{24,16},{1,9},{9,1},{17,25},{25,17},{2,10},{10... | collective-permute-start | bytes 1671176 | tf_op jit(solution)/shard_map/ppermute | solution.py:20
  166.6 16.3 %collective-permute-start.27 = (bf16[256,1088]{0,1:T(8,128)(2,1)}, bf16[256,1088]{0,1:T(8,128)(2,1)}, u32[]{:S(2)}, u32[]{:S(2)}) collective-permute-start(bf16[256,1088]{0,1:T(8,128)(2,1)} %copy.124), channel_id=1, source_target_pairs={{0,16},{8,24},{16,0},{24,8},{1,17},{9,25},{17,1},{25,9},{2,18},{10... | collective-permute-start | bytes 1671176 | tf_op jit(solution)/shard_map/ppermute | solution.py:20
  168.1 21.6 %collective-permute-start.7 = (bf16[256,1088]{0,1:T(8,128)(2,1)S(1)}, bf16[256,1088]{0,1:T(8,128)(2,1)S(1)}, u32[]{:S(2)}, u32[]{:S(2)}) collective-permute-start(bf16[256,1088]{0,1:T(8,128)(2,1)S(1)} %copy.94), channel_id=1, source_target_pairs={{0,8},{8,0},{16,24},{24,16},{1,9},{9,1},{17,25},{25,17},{2,10},{10... | collective-permute-start | bytes 1671176 | tf_op jit(solution)/shard_map/ppermute | solution.py:20
  174.5 18.1 %collective-permute-start.8 = (bf16[256,1088]{0,1:T(8,128)(2,1)S(1)}, bf16[256,1088]{0,1:T(8,128)(2,1)}, u32[]{:S(2)}, u32[]{:S(2)}) collective-permute-start(bf16[256,1088]{0,1:T(8,128)(2,1)S(1)} %copy.94), channel_id=1, source_target_pairs={{0,16},{8,24},{16,0},{24,8},{1,17},{9,25},{17,1},{25,9},{2,18},{10... | collective-permute-start | bytes 1671176 | tf_op jit(solution)/shard_map/ppermute | solution.py:20
  185.0 12.2 %collective-permute-start.28 = (bf16[128,1088]{1,0:T(8,128)(2,1)}, bf16[128,1088]{1,0:T(8,128)(2,1)}, u32[]{:S(2)}, u32[]{:S(2)}) collective-permute-start(bf16[128,1088]{1,0:T(8,128)(2,1)} %slice.547), channel_id=1, source_target_pairs={{0,8},{8,0},{16,24},{24,16},{1,9},{9,1},{17,25},{25,17},{2,10},{10... | collective-permute-start | bytes 835592 | tf_op jit(solution)/shard_map/ppermute | solution.py:20
  185.8 13.2 %collective-permute-start.29 = (bf16[128,1088]{1,0:T(8,128)(2,1)}, bf16[128,1088]{1,0:T(8,128)(2,1)}, u32[]{:S(2)}, u32[]{:S(2)}) collective-permute-start(bf16[128,1088]{1,0:T(8,128)(2,1)} %slice.548), channel_id=1, source_target_pairs={{0,16},{8,24},{16,0},{24,8},{1,17},{9,25},{17,1},{25,9},{2,18},{10... | collective-permute-start | bytes 835592 | tf_op jit(solution)/shard_map/ppermute | solution.py:20
  194.9 32.0 %collective-permute-start.9 = (bf16[128,1088]{1,0:T(8,128)(2,1)S(1)}, bf16[128,1088]{1,0:T(8,128)(2,1)S(1)}, u32[]{:S(2)}, u32[]{:S(2)}) collective-permute-start(bf16[128,1088]{1,0:T(8,128)(2,1)S(1)} %slice.539), channel_id=1, source_target_pairs={{0,8},{8,0},{16,24},{24,16},{1,9},{9,1},{17,25},{25,17},{2,10},{10... | collective-permute-start | bytes 835592 | tf_op jit(solution)/shard_map/ppermute | solution.py:20
  196.6 31.1 %collective-permute-start.10 = (bf16[128,1088]{1,0:T(8,128)(2,1)S(1)}, bf16[128,1088]{1,0:T(8,128)(2,1)S(1)}, u32[]{:S(2)}, u32[]{:S(2)}) collective-permute-start(bf16[128,1088]{1,0:T(8,128)(2,1)S(1)} %slice.540), channel_id=1, source_target_pairs={{0,16},{8,24},{16,0},{24,8},{1,17},{9,25},{17,1},{25,9},{2,18},{10... | collective-permute-start | bytes 835592 | tf_op jit(solution)/shard_map/ppermute | solution.py:20
  255.5 239.7 %reduce-scatter.19.cloned.1.call-start = ((), (), s32[]{:S(2)}) async-start(), calls=%async_computation.11 | async-start | bytes 2820096
  257.8 46.7 %collective-permute-start.15 = (bf16[128,1088]{1,0:T(8,128)(2,1)}, bf16[128,1088]{1,0:T(8,128)(2,1)}, u32[]{:S(2)}, u32[]{:S(2)}) collective-permute-start(bf16[128,1088]{1,0:T(8,128)(2,1)} %get-tuple-element.166), channel_id=1, source_target_pairs={{0,16},{8,24},{16,0},{24,8},{1,17},{9,25},{17,1},{25,9},{2,18},{10... | collective-permute-start | bytes 835592 | tf_op jit(solution)/shard_map/ppermute | solution.py:20
  259.2 46.7 %collective-permute-start.17 = (bf16[128,1088]{1,0:T(8,128)(2,1)}, bf16[128,1088]{1,0:T(8,128)(2,1)}, u32[]{:S(2)}, u32[]{:S(2)}) collective-permute-start(bf16[128,1088]{1,0:T(8,128)(2,1)} %get-tuple-element.165), channel_id=1, source_target_pairs={{0,8},{8,0},{16,24},{24,16},{1,9},{9,1},{17,25},{25,17},{2,10},{10... | collective-permute-start | bytes 835592 | tf_op jit(solution)/shard_map/ppermute | solution.py:20
  261.6 17.9 %collective-permute-start.49 = (bf16[128,1088]{1,0:T(8,128)(2,1)S(1)}, bf16[128,1088]{1,0:T(8,128)(2,1)}, u32[]{:S(2)}, u32[]{:S(2)}) collective-permute-start(bf16[128,1088]{1,0:T(8,128)(2,1)S(1)} %get-tuple-element.160), channel_id=1, source_target_pairs={{0,16},{8,24},{16,0},{24,8},{1,17},{9,25},{17,1},{25,9},{2,18},{10... | collective-permute-start | bytes 835592 | tf_op jit(solution)/shard_map/ppermute | solution.py:20
  263.1 16.8 %collective-permute-start.51 = (bf16[128,1088]{1,0:T(8,128)(2,1)S(1)}, bf16[128,1088]{1,0:T(8,128)(2,1)}, u32[]{:S(2)}, u32[]{:S(2)}) collective-permute-start(bf16[128,1088]{1,0:T(8,128)(2,1)S(1)} %get-tuple-element.159), channel_id=1, source_target_pairs={{0,8},{8,0},{16,24},{24,16},{1,9},{9,1},{17,25},{25,17},{2,10},{10... | collective-permute-start | bytes 835592 | tf_op jit(solution)/shard_map/ppermute | solution.py:20
  264.9 19.6 %collective-permute-start.38 = (bf16[128,1088]{1,0:T(8,128)(2,1)}, bf16[128,1088]{1,0:T(8,128)(2,1)}, u32[]{:S(2)}, u32[]{:S(2)}) collective-permute-start(bf16[128,1088]{1,0:T(8,128)(2,1)} %get-tuple-element.154), channel_id=1, source_target_pairs={{0,16},{8,24},{16,0},{24,8},{1,17},{9,25},{17,1},{25,9},{2,18},{10... | collective-permute-start | bytes 835592 | tf_op jit(solution)/shard_map/ppermute | solution.py:20
  277.0 240.6 %reduce-scatter.13.cloned.1.call-start = ((), (), s32[]{:S(2)}) async-start(), calls=%async_computation.8 | async-start | bytes 2506752
  279.9 15.9 %collective-permute-start.34 = (bf16[128,1088]{1,0:T(8,128)(2,1)}, bf16[128,1088]{1,0:T(8,128)(2,1)}, u32[]{:S(2)}, u32[]{:S(2)}) collective-permute-start(bf16[128,1088]{1,0:T(8,128)(2,1)} %get-tuple-element.172), channel_id=1, source_target_pairs={{0,16},{8,24},{16,0},{24,8},{1,17},{9,25},{17,1},{25,9},{2,18},{10... | collective-permute-start | bytes 835592 | tf_op jit(solution)/shard_map/ppermute | solution.py:20
  284.5 12.7 %collective-permute-start.36 = (bf16[128,1088]{1,0:T(8,128)(2,1)}, bf16[128,1088]{1,0:T(8,128)(2,1)}, u32[]{:S(2)}, u32[]{:S(2)}) collective-permute-start(bf16[128,1088]{1,0:T(8,128)(2,1)} %get-tuple-element.171), channel_id=1, source_target_pairs={{0,8},{8,0},{16,24},{24,16},{1,9},{9,1},{17,25},{25,17},{2,10},{10... | collective-permute-start | bytes 835592 | tf_op jit(solution)/shard_map/ppermute | solution.py:20
  289.0 21.9 %collective-permute-start.50 = (bf16[256,1088]{0,1:T(8,128)(2,1)}, bf16[256,1088]{0,1:T(8,128)(2,1)}, u32[]{:S(2)}, u32[]{:S(2)}) collective-permute-start(bf16[256,1088]{0,1:T(8,128)(2,1)} %copy.152), channel_id=1, source_target_pairs={{0,8},{8,0},{16,24},{24,16},{1,9},{9,1},{17,25},{25,17},{2,10},{10... | collective-permute-start | bytes 1671176 | tf_op jit(solution)/shard_map/ppermute | solution.py:20
  295.8 18.9 %collective-permute-start.52 = (bf16[256,1088]{0,1:T(8,128)(2,1)}, bf16[256,1088]{0,1:T(8,128)(2,1)}, u32[]{:S(2)}, u32[]{:S(2)}) collective-permute-start(bf16[256,1088]{0,1:T(8,128)(2,1)} %copy.154), channel_id=1, source_target_pairs={{0,16},{8,24},{16,0},{24,8},{1,17},{9,25},{17,1},{25,9},{2,18},{10... | collective-permute-start | bytes 1671176 | tf_op jit(solution)/shard_map/ppermute | solution.py:20
  297.2 22.0 %collective-permute-start.39 = (bf16[256,1088]{0,1:T(8,128)(2,1)}, bf16[256,1088]{0,1:T(8,128)(2,1)}, u32[]{:S(2)}, u32[]{:S(2)}) collective-permute-start(bf16[256,1088]{0,1:T(8,128)(2,1)} %copy.141), channel_id=1, source_target_pairs={{0,8},{8,0},{16,24},{24,16},{1,9},{9,1},{17,25},{25,17},{2,10},{10... | collective-permute-start | bytes 1671176 | tf_op jit(solution)/shard_map/ppermute | solution.py:20
  304.6 18.6 %collective-permute-start.41 = (bf16[256,1088]{0,1:T(8,128)(2,1)}, bf16[256,1088]{0,1:T(8,128)(2,1)}, u32[]{:S(2)}, u32[]{:S(2)}) collective-permute-start(bf16[256,1088]{0,1:T(8,128)(2,1)} %copy.143), channel_id=1, source_target_pairs={{0,16},{8,24},{16,0},{24,8},{1,17},{9,25},{17,1},{25,9},{2,18},{10... | collective-permute-start | bytes 1671176 | tf_op jit(solution)/shard_map/ppermute | solution.py:20
  305.9 22.6 %collective-permute-start.35 = (bf16[256,1088]{0,1:T(8,128)(2,1)}, bf16[256,1088]{0,1:T(8,128)(2,1)}, u32[]{:S(2)}, u32[]{:S(2)}) collective-permute-start(bf16[256,1088]{0,1:T(8,128)(2,1)} %copy.137), channel_id=1, source_target_pairs={{0,8},{8,0},{16,24},{24,16},{1,9},{9,1},{17,25},{25,17},{2,10},{10... | collective-permute-start | bytes 1671176 | tf_op jit(solution)/shard_map/ppermute | solution.py:20
  310.9 32.5 %collective-permute-start.16 = (bf16[256,1088]{0,1:T(8,128)(2,1)}, bf16[256,1088]{0,1:T(8,128)(2,1)}, u32[]{:S(2)}, u32[]{:S(2)}) collective-permute-start(bf16[256,1088]{0,1:T(8,128)(2,1)} %copy.109), channel_id=1, source_target_pairs={{0,8},{8,0},{16,24},{24,16},{1,9},{9,1},{17,25},{25,17},{2,10},{10... | collective-permute-start | bytes 1671176 | tf_op jit(solution)/shard_map/ppermute | solution.py:20
  314.7 30.8 %collective-permute-start.18 = (bf16[256,1088]{0,1:T(8,128)(2,1)}, bf16[256,1088]{0,1:T(8,128)(2,1)}, u32[]{:S(2)}, u32[]{:S(2)}) collective-permute-start(bf16[256,1088]{0,1:T(8,128)(2,1)} %copy.111), channel_id=1, source_target_pairs={{0,16},{8,24},{16,0},{24,8},{1,17},{9,25},{17,1},{25,9},{2,18},{10... | collective-permute-start | bytes 1671176 | tf_op jit(solution)/shard_map/ppermute | solution.py:20
  319.2 16.2 %collective-permute-start.37 = (bf16[256,1088]{0,1:T(8,128)(2,1)}, bf16[256,1088]{0,1:T(8,128)(2,1)}, u32[]{:S(2)}, u32[]{:S(2)}) collective-permute-start(bf16[256,1088]{0,1:T(8,128)(2,1)} %copy.139), channel_id=1, source_target_pairs={{0,16},{8,24},{16,0},{24,8},{1,17},{9,25},{17,1},{25,9},{2,18},{10... | collective-permute-start | bytes 1671176 | tf_op jit(solution)/shard_map/ppermute | solution.py:20
  359.0 21.6 %collective-permute-start.42 = (bf16[256,256]{1,0:T(8,128)(2,1)S(1)}, bf16[256,256]{1,0:T(8,128)(2,1)S(1)}, u32[]{:S(2)}, u32[]{:S(2)}) collective-permute-start(bf16[256,256]{1,0:T(8,128)(2,1)S(1)} %get-tuple-element.208), channel_id=1, source_target_pairs={{0,8},{8,0},{16,24},{24,16},{1,9},{9,1},{17,25},{25,17},{2,10},{10... | collective-permute-start | bytes 393224 | tf_op jit(solution)/shard_map/ppermute | solution.py:20
  360.4 20.2 %collective-permute-start.43 = (bf16[256,256]{1,0:T(8,128)(2,1)S(1)}, bf16[256,256]{1,0:T(8,128)(2,1)S(1)}, u32[]{:S(2)}, u32[]{:S(2)}) collective-permute-start(bf16[256,256]{1,0:T(8,128)(2,1)S(1)} %get-tuple-element.207), channel_id=1, source_target_pairs={{0,16},{8,24},{16,0},{24,8},{1,17},{9,25},{17,1},{25,9},{2,18},{10... | collective-permute-start | bytes 393224 | tf_op jit(solution)/shard_map/ppermute | solution.py:20
  361.6 19.0 %collective-permute-start.44 = (bf16[256,256]{1,0:T(8,128)(2,1)S(1)}, bf16[256,256]{1,0:T(8,128)(2,1)S(1)}, u32[]{:S(2)}, u32[]{:S(2)}) collective-permute-start(bf16[256,256]{1,0:T(8,128)(2,1)S(1)} %get-tuple-element.206), channel_id=1, source_target_pairs={{0,24},{8,16},{16,8},{24,0},{1,25},{9,17},{17,9},{25,1},{2,26},{10... | collective-permute-start | bytes 393224 | tf_op jit(solution)/shard_map/ppermute | solution.py:20
  443.0 110.2 %reduce-scatter.15.cloned.1.call-start = ((), (), s32[]{:S(2)}) async-start(), calls=%async_computation.9 | async-start | bytes 2820096
  447.2 10.0 %collective-permute-start.56 = (bf16[128,1088]{1,0:T(8,128)(2,1)S(1)}, bf16[128,1088]{1,0:T(8,128)(2,1)S(1)}, u32[]{:S(2)}, u32[]{:S(2)}) collective-permute-start(bf16[128,1088]{1,0:T(8,128)(2,1)S(1)} %get-tuple-element.142), channel_id=1, source_target_pairs={{0,16},{8,24},{16,0},{24,8},{1,17},{9,25},{17,1},{25,9},{2,18},{10... | collective-permute-start | bytes 835592 | tf_op jit(solution)/shard_map/ppermute | solution.py:20
  449.0 14.5 %collective-permute-start.45 = (bf16[128,1088]{1,0:T(8,128)(2,1)S(1)}, bf16[128,1088]{1,0:T(8,128)(2,1)S(1)}, u32[]{:S(2)}, u32[]{:S(2)}) collective-permute-start(bf16[128,1088]{1,0:T(8,128)(2,1)S(1)} %get-tuple-element.148), channel_id=1, source_target_pairs={{0,16},{8,24},{16,0},{24,8},{1,17},{9,25},{17,1},{25,9},{2,18},{10... | collective-permute-start | bytes 835592 | tf_op jit(solution)/shard_map/ppermute | solution.py:20
  450.2 13.3 %collective-permute-start.47 = (bf16[128,1088]{1,0:T(8,128)(2,1)S(1)}, bf16[128,1088]{1,0:T(8,128)(2,1)}, u32[]{:S(2)}, u32[]{:S(2)}) collective-permute-start(bf16[128,1088]{1,0:T(8,128)(2,1)S(1)} %get-tuple-element.147), channel_id=1, source_target_pairs={{0,8},{8,0},{16,24},{24,16},{1,9},{9,1},{17,25},{25,17},{2,10},{10... | collective-permute-start | bytes 835592 | tf_op jit(solution)/shard_map/ppermute | solution.py:20
  459.4 17.2 %collective-permute-start.57 = (bf16[256,1088]{0,1:T(8,128)(2,1)}, bf16[256,1088]{0,1:T(8,128)(2,1)}, u32[]{:S(2)}, u32[]{:S(2)}) collective-permute-start(bf16[256,1088]{0,1:T(8,128)(2,1)} %copy.159), channel_id=1, source_target_pairs={{0,8},{8,0},{16,24},{24,16},{1,9},{9,1},{17,25},{25,17},{2,10},{10... | collective-permute-start | bytes 1671176 | tf_op jit(solution)/shard_map/ppermute | solution.py:20
  461.3 16.7 %collective-permute-start.59 = (bf16[256,1088]{0,1:T(8,128)(2,1)}, bf16[256,1088]{0,1:T(8,128)(2,1)}, u32[]{:S(2)}, u32[]{:S(2)}) collective-permute-start(bf16[256,1088]{0,1:T(8,128)(2,1)} %copy.161), channel_id=1, source_target_pairs={{0,16},{8,24},{16,0},{24,8},{1,17},{9,25},{17,1},{25,9},{2,18},{10... | collective-permute-start | bytes 1671176 | tf_op jit(solution)/shard_map/ppermute | solution.py:20
  466.0 14.1 %collective-permute-start.46 = (bf16[256,1088]{0,1:T(8,128)(2,1)}, bf16[256,1088]{0,1:T(8,128)(2,1)}, u32[]{:S(2)}, u32[]{:S(2)}) collective-permute-start(bf16[256,1088]{0,1:T(8,128)(2,1)} %copy.148), channel_id=1, source_target_pairs={{0,8},{8,0},{16,24},{24,16},{1,9},{9,1},{17,25},{25,17},{2,10},{10... | collective-permute-start | bytes 1671176 | tf_op jit(solution)/shard_map/ppermute | solution.py:20
  467.9 14.3 %collective-permute-start.48 = (bf16[256,1088]{0,1:T(8,128)(2,1)}, bf16[256,1088]{0,1:T(8,128)(2,1)}, u32[]{:S(2)}, u32[]{:S(2)}) collective-permute-start(bf16[256,1088]{0,1:T(8,128)(2,1)} %copy.150), channel_id=1, source_target_pairs={{0,16},{8,24},{16,0},{24,8},{1,17},{9,25},{17,1},{25,9},{2,18},{10... | collective-permute-start | bytes 1671176 | tf_op jit(solution)/shard_map/ppermute | solution.py:20
  495.1 11.4 %collective-permute-start.71 = (bf16[136,1088]{1,0:T(8,128)(2,1)}, bf16[136,1088]{1,0:T(8,128)(2,1)S(1)}, u32[]{:S(2)}, u32[]{:S(2)}) collective-permute-start(bf16[136,1088]{1,0:T(8,128)(2,1)} %reduce-scatter.19.cloned.1.call-done), channel_id=1, source_target_pairs={{0,16},{8,24},{16,0},{24,8},{1,17},{9,25},{17,1},{25,9},{2,18},{10... | collective-permute-start | bytes 887816 | tf_op jit(solution)/shard_map/ppermute | solution.py:20
  496.8 11.2 %collective-permute-start.70 = (bf16[136,1088]{1,0:T(8,128)(2,1)}, bf16[136,1088]{1,0:T(8,128)(2,1)S(1)}, u32[]{:S(2)}, u32[]{:S(2)}) collective-permute-start(bf16[136,1088]{1,0:T(8,128)(2,1)} %reduce-scatter.19.cloned.1.call-done), channel_id=1, source_target_pairs={{0,8},{8,0},{16,24},{24,16},{1,9},{9,1},{17,25},{25,17},{2,10},{10... | collective-permute-start | bytes 887816 | tf_op jit(solution)/shard_map/ppermute | solution.py:20
  497.0 12.9 %collective-permute-start.68 = (bf16[68,1088]{1,0:T(8,128)(2,1)S(1)}, bf16[68,1088]{1,0:T(8,128)(2,1)S(1)}, u32[]{:S(2)}, u32[]{:S(2)}) collective-permute-start(bf16[68,1088]{1,0:T(8,128)(2,1)S(1)} %slice.586), channel_id=1, source_target_pairs={{0,8},{8,0},{16,24},{24,16},{1,9},{9,1},{17,25},{25,17},{2,10},{10... | collective-permute-start | bytes 443912 | tf_op jit(solution)/shard_map/ppermute | solution.py:20
  527.8 25.4 %collective-permute-start.62 = (bf16[68,972]{0,1:T(8,128)(2,1)S(1)}, bf16[68,972]{0,1:T(8,128)(2,1)S(1)}, u32[]{:S(2)}, u32[]{:S(2)}) collective-permute-start(bf16[68,972]{0,1:T(8,128)(2,1)S(1)} %slice.569), channel_id=1, source_target_pairs={{0,8},{8,0},{16,24},{24,16},{1,9},{9,1},{17,25},{25,17},{2,10},{10... | collective-permute-start | bytes 396584 | tf_op jit(solution)/shard_map/ppermute | solution.py:20
  530.2 23.0 %collective-permute-start.63 = (bf16[68,972]{0,1:T(8,128)(2,1)S(1)}, bf16[68,972]{0,1:T(8,128)(2,1)S(1)}, u32[]{:S(2)}, u32[]{:S(2)}) collective-permute-start(bf16[68,972]{0,1:T(8,128)(2,1)S(1)} %slice.570), channel_id=1, source_target_pairs={{0,16},{8,24},{16,0},{24,8},{1,17},{9,25},{17,1},{25,9},{2,18},{10... | collective-permute-start | bytes 396584 | tf_op jit(solution)/shard_map/ppermute | solution.py:20
  (110 other events, 1265.9 us)
Sparse Core Ops, SparseCore 0:
  16.8 32.8 all-gather.4
  51.3 32.3 all-gather.6
  85.4 31.9 all-gather.10
  118.9 31.9 all-gather.8
  255.6 38.4 reduce-scatter.16
  297.0 37.3 reduce-scatter.18
  443.1 35.9 reduce-scatter.12
  481.6 37.3 reduce-scatter.14
